TPU v7x, 128 devices: a whole 4x4x4 slice. The times are simulated.
128 devices in a mesh: group: 8 (over x_hi, y), resp: 16 (over z, x_lo, core).
Axes of the slice: x: 4 (x_hi: 2, x_lo: 2; x = x_hi * 2 + x_lo), y: 4, z: 4, core: 2. Of those that a mesh axis runs over, the one named last changes fastest.
Arguments:
- query_raw: bfloat16 [8, 16, 256, 4096], P('group', 'resp')
- key_raw: bfloat16 [8, 16, 256, 512], P('group', 'resp')
- response_values: bfloat16 [8, 16, 256, 512], P('group', 'resp'), may hold values from -6 to 6
- prompt_keys: bfloat16 [8, 16, 1792, 512], P('group', 'resp'), may hold values from -6 to 6
- prompt_values: bfloat16 [8, 16, 1792, 512], P('group', 'resp'), may hold values from -6 to 6
- grad_output: bfloat16 [8, 16, 256, 4096], P('group', 'resp'), may hold values from -6 to 6
- query_gain: float32 [128], replicated, may hold values from 0.6 to 6
- key_gain: float32 [128], replicated, may hold values from 0.6 to 6
- lengths: int32 [8, 16], P('group', 'resp'), may hold values from 1 to 256, as said below
- owner: int32 [8], P('group'), may hold values from 0 to 15
Outputs:
- query_grad: bfloat16 [8, 16, 256, 4096], P('group', 'resp')
- key_grad: bfloat16 [8, 16, 256, 512], P('group', 'resp')
- value_grad: bfloat16 [8, 16, 256, 512], P('group', 'resp')
- prompt_key_grad: bfloat16 [8, 16, 1792, 512], P('group', 'resp')
- prompt_value_grad: bfloat16 [8, 16, 1792, 512], P('group', 'resp')
- gain_grads: float32 [2, 128], replicated
Inputs may be any that keep to these rules, and one draw needn't show every extreme that they name: `lengths`: some response of every group has all 256 tokens live.
All inputs are finite; a program needn't handle non-finite values.
Results may differ from a plain program's by a relative error of at most 0.018.
The roundings to bfloat16 on the way count: a program that leaves them out, or rounds other values in their place, can miss the bound.
Values may be sent and summed in bfloat16 or wider, within the bound.
A program may use at most 128 MiB of HBM per device.

v0:
```python
import jax
import jax.numpy as jnp
from jax import lax
from jax.sharding import PartitionSpec as P

DH = 128


epsilon = 1e-06


def spread(value, axis, root):
    mine = lax.axis_index(axis) == root
    return lax.psum(jnp.where(mine, value, jnp.zeros_like(value)), axis)


def normalize(raw, gain):
    values = raw.astype(jnp.float32).reshape(raw.shape[0], -1, DH)
    inverse = lax.rsqrt(jnp.mean(values * values, axis=-1, keepdims=True) + epsilon)
    unit = values * inverse
    return (unit, inverse, (unit * gain).astype(jnp.bfloat16))


def norm_back(grad_normed, unit, inverse, gain):
    grad_unit = grad_normed * gain
    grad_raw = (grad_unit - unit * jnp.mean(grad_unit * unit, axis=-1, keepdims=True)) * inverse
    return (grad_raw.reshape(grad_raw.shape[0], -1), jnp.sum(grad_normed * unit, axis=(0, 1)))


def attend_back(queries, key_rows, value_rows, grad_out):
    count = queries.shape[0]
    total = key_rows.shape[0]
    heads = queries.shape[1] // DH
    kv_heads = key_rows.shape[1] // DH
    pairs_per = heads // kv_heads // 2
    allowed = (
        jnp.arange(total, dtype=jnp.int32)[None, :] - (total - count)
        <= jnp.arange(count, dtype=jnp.int32)[:, None]
    )[None]
    factor = DH ** (-0.5)
    query_pairs = jnp.moveaxis(queries.reshape(count, heads // 2, 2, DH), 1, 0)
    out_pairs = jnp.moveaxis(grad_out.reshape(count, heads // 2, 2, DH), 1, 0)
    key_heads = key_rows.reshape(total, kv_heads, DH)
    value_heads = value_rows.reshape(total, kv_heads, DH)

    def one_pair(carry, items):
        grad_keys, grad_values = carry
        pair_index, query_pair, out_pair = items
        shared = pair_index // pairs_per
        key_block = lax.dynamic_index_in_dim(key_heads, shared, 1, keepdims=False)
        value_block = lax.dynamic_index_in_dim(value_heads, shared, 1, keepdims=False)
        scores = (
            jnp.einsum("rhd,kd->hrk", query_pair, key_block, preferred_element_type=jnp.float32)
            * factor
        )
        scores = jnp.where(allowed, scores, -jnp.inf)
        peak = jnp.max(scores, axis=-1, keepdims=True)
        exponent = jnp.exp(scores - peak)
        probs = exponent / jnp.sum(exponent, axis=-1, keepdims=True)
        probs_low = probs.astype(jnp.bfloat16)
        outputs = jnp.einsum(
            "hrk,kd->rhd", probs_low, value_block, preferred_element_type=jnp.float32
        )
        row_dots = jnp.sum(out_pair.astype(jnp.float32) * outputs, axis=-1)
        grad_probs = jnp.einsum(
            "rhd,kd->hrk", out_pair, value_block, preferred_element_type=jnp.float32
        )
        grad_scores = (probs * (grad_probs - jnp.transpose(row_dots)[:, :, None]) * factor).astype(
            jnp.bfloat16
        )
        grad_query = jnp.einsum(
            "hrk,kd->rhd", grad_scores, key_block, preferred_element_type=jnp.float32
        )
        key_add = jnp.einsum(
            "hrk,rhd->kd", grad_scores, query_pair, preferred_element_type=jnp.float32
        )
        value_add = jnp.einsum(
            "hrk,rhd->kd", probs_low, out_pair, preferred_element_type=jnp.float32
        )
        grad_keys = grad_keys.at[shared].add(key_add)
        grad_values = grad_values.at[shared].add(value_add)
        return ((grad_keys, grad_values), grad_query)

    empty = jnp.zeros((kv_heads, total, DH), jnp.float32)
    steps_index = jnp.arange(heads // 2, dtype=jnp.int32)
    (grad_keys, grad_values), grad_queries = lax.scan(
        one_pair, (empty, empty), (steps_index, query_pairs, out_pairs)
    )
    grad_queries = jnp.moveaxis(grad_queries, 0, 1).reshape(count, heads, DH)
    return (grad_queries, jnp.moveaxis(grad_keys, 0, 1), jnp.moveaxis(grad_values, 0, 1))


def body(
    query_raw,
    key_raw,
    response_values,
    prompt_keys,
    prompt_values,
    grad_output,
    query_gain,
    key_gain,
    lengths,
    owner,
):
    count = query_raw.shape[2]
    prompt_rows = prompt_keys.shape[2]
    width = prompt_keys.shape[3]
    members = lax.axis_size("resp")
    leader = owner[0]
    is_leader = lax.axis_index("resp") == leader
    live_total = lax.psum(lengths.astype(jnp.float32), "resp")
    scaling = members * count / live_total[0, 0]
    prompt_key, prompt_value = (
        spread(prompt_keys[0, 0], "resp", leader),
        spread(prompt_values[0, 0], "resp", leader),
    )
    p_unit, p_inverse, p_normed = normalize(prompt_key, key_gain)
    query_unit, query_inverse, query_normed = normalize(query_raw[0, 0], query_gain)
    key_unit, key_inverse, key_normed = normalize(key_raw[0, 0], key_gain)
    live = (jnp.arange(count, dtype=jnp.int32) < lengths[0, 0])[:, None]
    grad_out = (grad_output[0, 0].astype(jnp.float32) * live * scaling).astype(jnp.bfloat16)
    key_rows = jnp.concatenate([p_normed, key_normed], axis=0).reshape(prompt_rows + count, width)
    value_rows = jnp.concatenate([prompt_value, response_values[0, 0]], axis=0)
    grad_query, grad_keys, grad_values = attend_back(
        query_normed.reshape(count, -1), key_rows, value_rows, grad_out
    )
    query_grad, query_part = norm_back(grad_query, query_unit, query_inverse, query_gain)
    key_grad, key_part = norm_back(grad_keys[prompt_rows:], key_unit, key_inverse, key_gain)
    value_grad = grad_values[prompt_rows:].reshape(count, width)
    key_sum = grad_keys[:prompt_rows].reshape(prompt_rows, width)
    value_sum = grad_values[:prompt_rows].reshape(prompt_rows, width)
    key_total, value_total = lax.psum((key_sum, value_sum), "resp")
    finished, extra = norm_back(key_total.reshape(prompt_rows, -1, DH), p_unit, p_inverse, key_gain)
    key_part = key_part + jnp.where(is_leader, extra, jnp.zeros_like(extra))
    key_low = finished.astype(jnp.bfloat16)
    value_low = value_total.astype(jnp.bfloat16)
    blank = jnp.zeros((), jnp.bfloat16)
    prompt_key_grad = jnp.where(is_leader, key_low, blank)
    prompt_value_grad = jnp.where(is_leader, value_low, blank)
    gains = lax.psum(jnp.stack([query_part, key_part]), ("group", "resp")) / (
        lax.axis_size("group") * members
    )
    return (
        query_grad.astype(jnp.bfloat16)[None, None],
        key_grad.astype(jnp.bfloat16)[None, None],
        value_grad.astype(jnp.bfloat16)[None, None],
        prompt_key_grad[None, None],
        prompt_value_grad[None, None],
        gains,
    )


def solution(mesh):
    in_specs = (
        P("group", "resp", None, None),
        P("group", "resp", None, None),
        P("group", "resp", None, None),
        P("group", "resp", None, None),
        P("group", "resp", None, None),
        P("group", "resp", None, None),
        P(),
        P(),
        P("group", "resp"),
        P("group"),
    )
    out_specs = (
        P("group", "resp", None, None),
        P("group", "resp", None, None),
        P("group", "resp", None, None),
        P("group", "resp", None, None),
        P("group", "resp", None, None),
        P(),
    )
    return jax.shard_map(body, mesh=mesh, in_specs=in_specs, out_specs=out_specs, check_vma=False)
```

profile of v0, /device:TPU:1, one launch (start us, length us, event | category | flops | bytes accessed | tf_op | source)
XLA Modules:
  0.0 1054.6 jit_solution(1436291300279022983)
XLA Ops:
  16.7 31.2 %psum.44 = f32[1,1]{1,0:T(1,128)} all-reduce(f32[1,1]{1,0:T(1,128)S(6)} %convert_element_type.129), channel_id=1, replica_groups=mesh['group'=8,'resp'=16] {'resp'}, use_global_device_ids=true, to_apply=%region_1.2 | all-reduce | flops 1 | bytes 8 | tf_op jit(solution)/shard_map/psum | solution.py:111
  64.5 5.0 mul.271
  71.3 5.3 fusion.66
  76.7 74.8 %all-reduce.7.cloned.1.call-done = (bf16[1792,512]{1,0:T(8,128)(2,1)}, bf16[1792,4,128]{2,0,1:T(8,128)(2,1)}) async-done(((bf16[1792,512]{1,0:T(8,128)(2,1)}, bf16[1792,4,128]{2,0,1:T(8,128)(2,1)}), (bf16[1792,512]{1,0:T(8,128)(2,1)}, bf16[1792,4,128]{2,0,1:T(8,128)(2,1)})) %all-reduce.7.cloned.1.call-update) | async-done | bytes 3670032 | tf_op jit(solution)/shard_map/psum | solution.py:14
  151.5 4.5 reshape.326
  156.1 4.6 multiply_reduce_fusion.1
  171.3 592.3 %while.19 = (s32[]{:T(128)}, f32[4,2048,128]{1,2,0:T(8,128)}, f32[4,2048,128]{2,1,0:T(8,128)}, f32[16,256,2,128]{1,3,2,0:T(8,128)}, s32[16]{0:T(128)}, /*index=5...) while((s32[]{:T(128)}, f32[4,2048,128]{1,2,0:T(8,128)}, ...), condition=%wide.region_11.12_spmd.clone, body=%wide.region_6.11_spmd.clone.sunk | while | flops 1623918080 | bytes 42360708 | solution.py:86
  175.6 4.4 fusion.126
  185.6 4.4 fusion.129
  195.3 3.9 fusion.130
  212.7 4.4 fusion.126
  222.7 4.4 fusion.129
  232.4 3.9 fusion.130
  249.8 4.4 fusion.126
  259.8 4.4 fusion.129
  269.5 3.9 fusion.130
  286.9 4.4 fusion.126
  296.9 4.4 fusion.129
  306.6 3.9 fusion.130
  323.9 4.4 fusion.126
  333.9 4.4 fusion.129
  343.6 3.9 fusion.130
  361.0 4.3 fusion.126
  371.0 4.4 fusion.129
  380.6 3.9 fusion.130
  398.0 4.3 fusion.126
  408.0 4.4 fusion.129
  417.7 3.9 fusion.130
  435.0 4.4 fusion.126
  445.0 4.4 fusion.129
  454.7 3.9 fusion.130
  472.0 4.4 fusion.126
  482.0 4.4 fusion.129
  491.7 3.9 fusion.130
  509.1 4.4 fusion.126
  519.0 4.4 fusion.129
  528.7 3.9 fusion.130
  546.0 4.4 fusion.126
  556.0 4.4 fusion.129
  565.7 3.9 fusion.130
  583.0 4.3 fusion.126
  593.0 4.4 fusion.129
  602.7 3.9 fusion.130
  620.0 4.3 fusion.126
  630.0 4.4 fusion.129
  639.7 3.9 fusion.130
  657.0 4.3 fusion.126
  667.0 4.4 fusion.129
  676.7 3.9 fusion.130
  694.0 4.3 fusion.126
  704.0 4.4 fusion.129
  731.0 4.3 fusion.126
  740.9 4.4 fusion.129
  763.6 4.2 slice.57
  767.9 5.1 copy.191
  773.0 4.4 copy_bitcast_fusion
  777.4 147.1 %all-reduce.8 = bf16[1792,512]{1,0:T(8,128)(2,1)} all-reduce(f32[1792,512]{1,0:T(8,128)} %copy_bitcast_fusion), channel_id=1, replica_groups=mesh['group'=8,'resp'=16] {'resp'}, use_global_device_ids=true, to_apply=%region_16.17 | all-reduce | flops 917504 | bytes 5505024 | tf_op jit(solution)/shard_map/psum | solution.py:132
  929.8 5.7 fusion.58
  938.1 5.0 mul.276
  943.1 5.6 copy.203
  951.1 7.5 multiply_convert_fusion
  960.9 4.0 multiply_reduce_fusion
  965.0 71.0 %psum.47 = f32[2,128]{1,0:T(2,128)S(1)} all-reduce(f32[2,128]{1,0:T(2,128)S(1)} %pad_maximum_fusion.2), channel_id=1, replica_groups=mesh['group'=8,'resp'=16] {'group','resp'}, use_global_device_ids=true, to_apply=%region_21.22 | all-reduce | flops 256 | bytes 2048 | tf_op jit(solution)/shard_map/psum | solution.py:140
  1042.7 5.0 fusion.69
  (316 shorter events, 410.6 us)
Async XLA Ops:
  7.2 144.3 %all-reduce.7.cloned.1.call-start = ((), (), s32[]{:S(2)}) async-start(), calls=%async_computation.1 | async-start | bytes 7340032 | tf_op jit(solution)/shard_map/psum | solution.py:14
  12.5 2.2 copy-start.6
  14.6 33.3 %copy-start.4 = (bf16[1,1,256,4096]{3,2,1,0:T(8,128)(2,1)S(1)}, bf16[1,1,256,4096]{3,2,1,0:T(8,128)(2,1)}, u32[]{:S(2)}) copy-start(bf16[1,1,256,4096]{3,2,1,0:T(8,128)(2,1)} %param.16) | copy-start | bytes 6291460
  16.0 942.7 %all-reduce.5.cloned.1.call-start = ((), (), s32[]{:S(2)}) async-start(), calls=%async_computation | async-start | bytes 7340032 | tf_op jit(solution)/shard_map/psum | solution.py:132
  54.0 3.7 copy-start.13
  54.0 3.9 copy-start.16
  54.0 4.2 copy-start.14
  57.6 13.7 %copy-start.11 = (f32[256,16,2]{0,2,1:T(2,128)}, f32[256,16,2]{0,2,1:T(2,128)S(1)}, u32[]{:S(2)}) copy-start(f32[256,16,2]{0,2,1:T(2,128)S(1)} %rsqrt.31) | copy-start | bytes 98308
  64.5 6.3 copy-start.19
  156.1 6.5 copy-start
  161.6 2.2 copy-start.7
  162.5 3.6 copy-start.8
  777.4 147.2 %copy-start.9 = (f32[1792,4]{0,1:T(4,128)S(1)}, f32[1792,4]{0,1:T(4,128)}, u32[]{:S(2)}) copy-start(f32[1792,4]{0,1:T(4,128)} %copy-done.8) | copy-start | bytes 86020
  777.4 152.3 %copy-start.12 = (f32[256,16,2]{0,2,1:T(2,128)S(1)}, f32[256,16,2]{0,2,1:T(2,128)}, u32[]{:S(2)}) copy-start(f32[256,16,2]{0,2,1:T(2,128)} %copy-done.11) | copy-start | bytes 98308
  777.4 152.3 %copy-start.20 = (f32[128]{0:T(128)S(1)}, f32[128]{0:T(128)}, u32[]{:S(2)}) copy-start(f32[128]{0:T(128)} %param.22) | copy-start | bytes 1540
  948.8 2.4 copy-start.5
  948.8 2.4 copy-start.15
  958.7 2.2 copy-start.1
  960.8 4.1 copy-start.3
  960.8 4.1 copy-start.21
  960.9 4.1 copy-start.22
  960.9 75.7 %copy-start.10 = (f32[1792,4]{0,1:T(4,128)S(1)}, f32[1792,4]{0,1:T(4,128)}, u32[]{:S(2)}) copy-start(f32[1792,4]{0,1:T(4,128)} %copy-done.8) | copy-start | bytes 86020
  960.9 75.6 %copy-start.17 = (f32[128]{0:T(128)S(1)}, f32[128]{0:T(128)}, u32[]{:S(2)}) copy-start(f32[128]{0:T(128)} %param.23) | copy-start | bytes 1540
  1040.1 2.6 copy-start.18
  1040.5 2.2 copy-start.2
Sparse Core Ops, SparseCore 0:
  16.1 135.3 all-reduce.6
  773.1 164.5 all-reduce.4
where the time goes:
time: 1060 us; the launch traced here: 1050 us
  matrix products  339 us (32%)
  blocking collectives  249 us (23%)
  local copies, waits for them, and re-layouts  210 us (20%)
  other arithmetic  122 us (12%)
  waiting for transfers between devices  74.9 us (7%)
  loops' own time  42.4 us (4%)
  between operations  16.4 us (2%)
    psum x1, blocking collectives, body(): key_total, value_total = lax.psum((key_sum, value_sum), 'resp')  147 us
    psum x1, waiting for transfers between devices, spread(): return lax.psum(jnp.where(mine, value, jnp.zeros_like(value)), axis)  74.8 us
    psum x1, blocking collectives, body(): lax.psum(jnp.stack([query_part, key_part]), ('group', 'resp'))  71 us
    dot_general x16, matrix products, one_pair(): jnp.einsum('rhd,kd->hrk', out_pair, value_block, preferred_element_type=j...  70.9 us
    sub x16, matrix products, one_pair(): exponent = jnp.exp(scores - peak)  69.6 us
    dot_general x16, matrix products, one_pair(): jnp.einsum('hrk,rhd->kd', grad_scores, query_pair, preferred_element_type...  62.1 us
    another operation x32, local copies, waits for them, and re-layouts  61.5 us
    dot_general x16, matrix products, one_pair(): jnp.einsum('hrk,rhd->kd', probs_low, out_pair, preferred_element_type=jnp...  56.7 us
  transfers between devices with their start and end apart: 2, of which 1 were waited for; matrix products, arithmetic and copies ran while one was open for 6% of the time, Pallas kernels for 0%

commit v1 on v0

--- a/solution.py
+++ b/solution.py
@@ -1,12 +1,496 @@
+import functools
+import math
+
 import jax
 import jax.numpy as jnp
 from jax import lax
+from jax.experimental import pallas as pl
+from jax.experimental.pallas import tpu as pltpu
 from jax.sharding import PartitionSpec as P
 
 DH = 128
-
-
-epsilon = 1e-06
+KVH = 4
+QH = 32
+L = 256
+PROMPT = 1792
+T = PROMPT + L
+RESPS = 16
+GROUPS = 8
+EPS = 1e-6
+HP = 2
+R = HP * L
+STEPS = QH // HP
+PER = STEPS // KVH
+FACT = DH ** -0.5
+C2 = FACT * math.log2(math.e)
+SUB = 32
+AC = 1024
+CH = 1024
+SAFE = 60.0
+f32 = jnp.float32
+bf16 = jnp.bfloat16
+MESH = pl.DeviceIdType.MESH
+
+
+def dot(a, b):
+    return jnp.dot(a, b, preferred_element_type=f32)
+
+
+def fold8(x):
+    return x.reshape(x.shape[0] // 8, 8, x.shape[1]).sum(0)
+
+
+def unit_of(x):
+    inv = lax.rsqrt(jnp.mean(x * x, axis=-1, keepdims=True) + EPS)
+    return x * inv, inv
+
+
+def norm_grad(grad, raw, gain):
+    unit, inv = unit_of(raw)
+    du = grad * gain
+    return (du - unit * jnp.mean(du * unit, axis=-1, keepdims=True)) * inv, fold8(grad * unit)
+
+
+HALF = PROMPT // 2
+SHARD = PROMPT // 16
+
+
+def place():
+    me = lax.axis_index("resp")
+    return me // 4, (me // 2) % 2, me % 2
+
+
+class Stream:
+    def __init__(self, z_first, acc, dst, r0, rz1, rz2, rx, send, recv):
+        z, x, c = place()
+        self.z_first, self.acc, self.dst = z_first, acc, dst
+        self.r0, self.rz1, self.rz2, self.rx, self.send, self.recv = r0, rz1, rz2, rx, send, recv
+        self.z, self.x, self.c = z, x, c
+        me = z * 4 + x * 2 + c
+        self.sib = z * 4 + x * 2 + (1 - c)
+        self.xp = z * 4 + (1 - x) * 2 + c
+        self.up = ((z + 1) % 4) * 4 + x * 2 + c
+        self.down = ((z + 3) % 4) * 4 + x * 2 + c
+        if z_first:
+            self.zn, self.za, self.xn = 2 * SHARD, SHARD, SHARD
+            self.zbase, self.xbase = c * HALF, c * HALF + z * 2 * SHARD
+            self.shard = c * HALF + z * 2 * SHARD + x * SHARD
+        else:
+            self.zn, self.za, self.xn = SHARD, 64, 4 * SHARD
+            self.zbase, self.xbase = c * HALF + x * 4 * SHARD, c * HALF
+            self.shard = c * HALF + x * 4 * SHARD + z * SHARD
+
+    def copy(self, h, slot, src, dst, who):
+        return pltpu.make_async_remote_copy(
+            src_ref=src, dst_ref=dst, send_sem=self.send.at[h, slot], recv_sem=self.recv.at[h, slot],
+            device_id={"resp": who}, device_id_type=MESH)
+
+    def rows(self, start, n):
+        return pl.ds(pl.multiple_of(start, 16), n)
+
+    def piece(self, k):
+        return self.zbase + ((self.z + k + 4) % 4) * self.zn
+
+    def add(self, h, start, n, *parts):
+        rows = self.rows(start, n)
+        total = self.acc[h, rows, :].astype(f32)
+        for part in parts:
+            total = total + part.astype(f32)
+        self.acc[h, rows, :] = total.astype(bf16)
+
+    def copies(self, h, name):
+        zn, za, xn, a, d = self.zn, self.za, self.xn, self.acc, self.dst
+        if name == "core":
+            return [self.copy(h, 0, a.at[h, self.rows((1 - self.c) * HALF, HALF), :], self.r0.at[h], self.sib)]
+        if name == "z1":
+            o = self.piece(2)
+            return [
+                self.copy(h, 1, a.at[h, self.rows(o, za), :], self.rz1.at[h, pl.ds(0, za), :], self.up),
+                self.copy(h, 2, a.at[h, self.rows(o + za, zn - za), :], self.rz1.at[h, pl.ds(za, zn - za), :], self.down)]
+        if name == "z2":
+            return [
+                self.copy(h, 3, a.at[h, self.rows(self.piece(1), zn), :], self.rz2.at[h, 0], self.up),
+                self.copy(h, 4, a.at[h, self.rows(self.piece(3), zn), :], self.rz2.at[h, 1], self.down)]
+        if name == "x":
+            return [self.copy(h, 5, a.at[h, self.rows(self.xbase + (1 - self.x) * xn, xn), :], self.rx.at[h], self.xp)]
+        if name == "gx":
+            r = self.rows(self.xbase + self.x * xn, xn)
+            return [self.copy(h, 6, d.at[h, r, :], d.at[h, r, :], self.xp)]
+        if name == "gz":
+            r = self.rows(self.piece(0), zn)
+            return [self.copy(h, 7, d.at[h, r, :], d.at[h, r, :], self.up),
+                    self.copy(h, 8, d.at[h, r, :], d.at[h, r, :], self.down)]
+        if name == "gf":
+            r, q = self.rows(self.piece(3), za), self.rows(self.piece(1) + za, zn - za)
+            return [self.copy(h, 9, d.at[h, r, :], d.at[h, r, :], self.up),
+                    self.copy(h, 10, d.at[h, q, :], d.at[h, q, :], self.down)]
+        r = self.rows(self.c * HALF, HALF)
+        return [self.copy(h, 11, d.at[h, r, :], d.at[h, r, :], self.sib)]
+
+    def start(self, h, name):
+        for one in self.copies(h, name):
+            one.start()
+
+    def wait(self, h, name):
+        for one in self.copies(h, name):
+            one.wait()
+
+    def combine(self, h, name):
+        zn, za = self.zn, self.za
+        if name == "core":
+            self.add(h, self.c * HALF, HALF, self.r0[h])
+        elif name == "z1":
+            self.add(h, self.piece(1), za, self.rz1[h, :za, :])
+            self.add(h, self.piece(3) + za, zn - za, self.rz1[h, za:, :])
+        elif name == "z2":
+            self.add(h, self.piece(0), zn, self.rz2[h, 0], self.rz2[h, 1])
+        elif name == "x":
+            self.add(h, self.xbase + self.x * self.xn, self.xn, self.rx[h])
+
+    def order(self):
+        if self.z_first:
+            return ["core", "z1", "z2", "x", "gx", "gz", "gf", "gcore"]
+        return ["core", "x", "z1", "z2", "gz", "gf", "gx", "gcore"]
+
+    def phase(self, h, k, finish):
+        names = self.order()
+        if k > 0:
+            self.wait(h, names[k - 1])
+            if k <= 4:
+                self.combine(h, names[k - 1])
+            if k == 4:
+                finish(h, self)
+        if k < 8:
+            self.start(h, names[k])
+
+
+PHASES = 9
+
+
+def stream_scratch(z_first):
+    zn, xn = (2 * SHARD, SHARD) if z_first else (SHARD, 4 * SHARD)
+    return [
+        pltpu.VMEM((KVH, HALF, DH), bf16),
+        pltpu.VMEM((KVH, zn, DH), bf16),
+        pltpu.VMEM((KVH, 2, zn, DH), bf16),
+        pltpu.VMEM((KVH, xn, DH), bf16),
+        pltpu.SemaphoreType.DMA((KVH, 12)),
+        pltpu.SemaphoreType.DMA((KVH, 12)),
+    ]
+
+
+def greet(barrier, peers_resp, peers_group):
+    for p in peers_resp:
+        pl.semaphore_signal(barrier, inc=1, device_id={"resp": p}, device_id_type=MESH)
+    for p in peers_group:
+        pl.semaphore_signal(barrier, inc=1, device_id={"group": p}, device_id_type=MESH)
+    pl.semaphore_wait(barrier, len(peers_resp) + len(peers_group))
+
+
+def others(axis, n):
+    me = lax.axis_index(axis)
+    return [(me + d) % n for d in range(1, n)]
+
+
+def exchange(axis, n, buf, send, recv):
+    me = lax.axis_index(axis)
+    copies = [
+        pltpu.make_async_remote_copy(
+            src_ref=buf.at[me], dst_ref=buf.at[me], send_sem=send.at[d - 1], recv_sem=recv.at[d - 1],
+            device_id={axis: (me + d) % n}, device_id_type=MESH)
+        for d in range(1, n)]
+    for one in copies:
+        one.start()
+    return copies
+
+
+def gather_kernel(kp, vp, kr, vr, kg, mine, ln, kn, vv, raw, live, acc_k, acc_v, lbuf, lsend, lrecv, *scratch):
+    keys = Stream(True, acc_k, kn, *scratch[:6])
+    values = Stream(False, acc_v, vv, *scratch[6:])
+    greet(pltpu.get_barrier_semaphore(), others("resp", RESPS), [])
+    me = lax.axis_index("resp")
+    lbuf[me] = jnp.zeros((8, DH), f32) + ln[0, 0].astype(f32)
+    small = exchange("resp", RESPS, lbuf, lsend, lrecv)
+    gain = kg[...]
+
+    def finish_keys(h, s):
+        rows = s.rows(s.shard, SHARD)
+        x = acc_k[h, rows, :]
+        raw[h] = x
+        unit, _ = unit_of(x.astype(f32))
+        kn[h, rows, :] = (unit * gain).astype(bf16)
+
+    def finish_values(h, s):
+        rows = s.rows(s.shard, SHARD)
+        vv[h, rows, :] = acc_v[h, rows, :]
+
+    flag = mine[0, 0] > 0
+    for h in range(KVH):
+        cols = slice(h * DH, (h + 1) * DH)
+        acc_k[h] = jnp.where(flag, kp[:, cols], jnp.zeros((), bf16))
+        acc_v[h] = jnp.where(flag, vp[:, cols], jnp.zeros((), bf16))
+        keys.phase(h, 0, None)
+        values.phase(h, 0, None)
+    for h in range(KVH):
+        cols = slice(h * DH, (h + 1) * DH)
+        unit, _ = unit_of(kr[:, cols].astype(f32))
+        kn[h, PROMPT:, :] = (unit * gain).astype(bf16)
+        vv[h, PROMPT:, :] = vr[:, cols]
+    for t in range(1, PHASES + KVH - 1):
+        for h in range(KVH):
+            if 1 <= t - h < PHASES:
+                keys.phase(h, t - h, finish_keys)
+                values.phase(h, t - h, finish_values)
+    for one in small:
+        one.wait()
+    live[...] = lbuf[...].sum(0)
+
+
+def gather(kp, vp, kr, vr, kg, mine, ln):
+    vm, sm = pl.BlockSpec(memory_space=pltpu.VMEM), pl.BlockSpec(memory_space=pltpu.SMEM)
+    return pl.pallas_call(
+        gather_kernel,
+        out_shape=(
+            jax.ShapeDtypeStruct((KVH, T, DH), bf16),
+            jax.ShapeDtypeStruct((KVH, T, DH), bf16),
+            jax.ShapeDtypeStruct((KVH, SHARD, DH), bf16),
+            jax.ShapeDtypeStruct((8, DH), f32),
+        ),
+        in_specs=[vm] * 5 + [sm] * 2,
+        out_specs=(vm,) * 4,
+        scratch_shapes=[
+            pltpu.VMEM((KVH, PROMPT, DH), bf16),
+            pltpu.VMEM((KVH, PROMPT, DH), bf16),
+            pltpu.VMEM((RESPS, 8, DH), f32),
+            pltpu.SemaphoreType.DMA((RESPS - 1,)),
+            pltpu.SemaphoreType.DMA((RESPS - 1,)),
+            *stream_scratch(True),
+            *stream_scratch(False),
+        ],
+        compiler_params=pltpu.CompilerParams(
+            collective_id=0, has_side_effects=True, vmem_limit_bytes=56 * 2**20),
+    )(kp, vp, kr, vr, kg, mine, ln)
+
+
+def prepare(h, q_ref, g_ref, gain, live, qt, gt):
+    cols = pl.ds(pl.multiple_of(h * DH, DH), DH)
+    rows = pl.ds(pl.multiple_of((h % HP) * L, L), L)
+    unit, _ = unit_of(q_ref[:, cols].astype(f32))
+    qt[h // HP, :, rows] = (unit * gain).T.astype(bf16)
+    gt[h // HP, :, rows] = (g_ref[:, cols].astype(f32) * live).T.astype(bf16)
+
+
+def front_chunk(c, kh, q, g, kn, vv, eb, dp, bias, l, rd):
+    x = dot(kn[kh, c * AC:(c + 1) * AC, :], q)
+    y = dot(vv[kh, c * AC:(c + 1) * AC, :], g)
+    for b in range(AC // SUB):
+        lo = c * AC + b * SUB
+        rows = slice(lo, lo + SUB)
+        xs = x[b * SUB:(b + 1) * SUB] * C2
+        if lo >= PROMPT:
+            xs = xs + bias[lo - PROMPT:lo - PROMPT + SUB, :]
+        ys = y[b * SUB:(b + 1) * SUB]
+        e = jnp.exp2(xs)
+        eb[rows, :] = e.astype(bf16)
+        dp[rows, :] = ys
+        l = l + fold8(e)
+        rd = rd + fold8(e * ys)
+    return l, rd
+
+
+def front_end(l, rd):
+    inv = 1.0 / jnp.sum(l, axis=0, keepdims=True)
+    return inv, jnp.sum(rd, axis=0, keepdims=True) * inv
+
+
+def back_begin(s, inv, qt, gt):
+    return (qt[s].astype(f32) * inv).T.astype(bf16), (gt[s].astype(f32) * inv).T.astype(bf16)
+
+
+def back_chunk(c, kh, rd, q, g, knt, eb, dp, ds, dk, dv, acc):
+    rows = slice(c * CH, (c + 1) * CH)
+    dv[kh, rows, :] += dot(eb[rows, :], g)
+    for b in range(CH // SUB):
+        r = slice(c * CH + b * SUB, c * CH + (b + 1) * SUB)
+        ds[r, :] = (eb[r, :].astype(f32) * (dp[r, :] - rd)).astype(bf16)
+    low = ds[rows, :]
+    dk[kh, rows, :] += dot(low, q)
+    t = dot(knt[kh, :, rows], low)
+    return t if acc is None else acc + t
+
+
+def finish_query(s, dqt, q_ref, gain, out, gpart):
+    for half in range(HP):
+        cols = pl.ds(pl.multiple_of((s * HP + half) * DH, DH), DH)
+        grad, term = norm_grad(dqt[:, half * L:(half + 1) * L].T, q_ref[:, cols].astype(f32), gain)
+        out[:, cols] = grad.astype(bf16)
+        gpart[...] += term
+
+
+def attend_kernel(q_ref, g_ref, kn, vv, kr, qg, kg, live_ref, ln, qo, ko, vo, dk_out, dv_out, part,
+                  qt, gt, knt, eb0, eb1, dp0, dp1, ds, bias, dk, dv, gpart):
+    q_gain, k_gain = qg[...], kg[...]
+    scale = RESPS * L / live_ref[0:1, 0:1]
+    live = jnp.where(lax.broadcasted_iota(jnp.int32, (L, 1), 0) < ln[0, 0], scale, 0.0)
+    key_row = lax.broadcasted_iota(jnp.int32, (L, R), 0)
+    query_row = lax.broadcasted_iota(jnp.int32, (L, R), 1) % L
+    bias[...] = jnp.where(key_row <= query_row, 0.0, -1e30)
+    gpart[...] = jnp.zeros_like(gpart)
+    dk[...] = jnp.zeros_like(dk)
+    dv[...] = jnp.zeros_like(dv)
+
+    def prep(h, _):
+        prepare(h, q_ref, g_ref, q_gain, live, qt, gt)
+        return 0
+    lax.fori_loop(0, QH, prep, 0)
+
+    def turn(i, _):
+        rows = pl.ds(pl.multiple_of(i * 256, 256), 256)
+        for h in range(KVH):
+            knt[h, :, rows] = kn[h, rows, :].astype(f32).T.astype(bf16)
+        return 0
+    lax.fori_loop(0, T // 256, turn, 0)
+
+    ebs, dps = (eb0, eb1), (dp0, dp1)
+    l = rd = jnp.zeros((8, R), f32)
+    for c in range(T // AC):
+        l, rd = front_chunk(c, 0, qt[0], gt[0], kn, vv, eb0, dp0, bias, l, rd)
+
+    def both(i, carry):
+        inv, rd = carry
+        for par in range(2):
+            s = 2 * i + par + 1
+            sn = jnp.minimum(s, STEPS - 1)
+            prev, now = par, 1 - par
+            q2, g2 = back_begin(s - 1, inv, qt, gt)
+            q, g = qt[sn], gt[sn]
+            l = r = jnp.zeros((8, R), f32)
+            acc = None
+            for c in range(T // AC):
+                l, r = front_chunk(c, sn // PER, q, g, kn, vv, ebs[now], dps[now], bias, l, r)
+                acc = back_chunk(c, (s - 1) // PER, rd, q2, g2, knt, ebs[prev], dps[prev], ds, dk, dv, acc)
+            finish_query(s - 1, acc * (inv * FACT), q_ref, q_gain, qo, gpart)
+            inv, rd = front_end(l, r)
+        return inv, rd
+    lax.fori_loop(0, STEPS // 2, both, front_end(l, rd))
+
+    terms = jnp.zeros((8, DH), f32)
+    for h in range(KVH):
+        cols = slice(h * DH, (h + 1) * DH)
+        grad, term = norm_grad(dk[h, PROMPT:, :] * FACT, kr[:, cols].astype(f32), k_gain)
+        ko[:, cols] = grad.astype(bf16)
+        vo[:, cols] = dv[h, PROMPT:, :].astype(bf16)
+        terms = terms + term
+    row = lax.broadcasted_iota(jnp.int32, (8, DH), 0)
+    query_term = jnp.sum(gpart[...], axis=0, keepdims=True)
+    key_term = jnp.sum(terms, axis=0, keepdims=True)
+    part[...] = jnp.where(row == 0, query_term, 0.0) + jnp.where(row == 1, key_term, 0.0)
+    dk_out[...] = (dk[:, :PROMPT, :] * FACT).astype(bf16)
+    dv_out[...] = dv[:, :PROMPT, :].astype(bf16)
+
+
+def attend(q, g, kn, vv, kr, qg, kg, live, ln):
+    vm, sm = pl.BlockSpec(memory_space=pltpu.VMEM), pl.BlockSpec(memory_space=pltpu.SMEM)
+    return pl.pallas_call(
+        attend_kernel,
+        out_shape=(
+            jax.ShapeDtypeStruct((L, QH * DH), bf16),
+            jax.ShapeDtypeStruct((L, KVH * DH), bf16),
+            jax.ShapeDtypeStruct((L, KVH * DH), bf16),
+            jax.ShapeDtypeStruct((KVH, PROMPT, DH), bf16),
+            jax.ShapeDtypeStruct((KVH, PROMPT, DH), bf16),
+            jax.ShapeDtypeStruct((8, DH), f32),
+        ),
+        in_specs=[vm] * 8 + [sm],
+        out_specs=(vm,) * 6,
+        scratch_shapes=[
+            pltpu.VMEM((STEPS, DH, R), bf16),
+            pltpu.VMEM((STEPS, DH, R), bf16),
+            pltpu.VMEM((KVH, DH, T), bf16),
+            pltpu.VMEM((T, R), bf16),
+            pltpu.VMEM((T, R), bf16),
+            pltpu.VMEM((T, R), f32),
+            pltpu.VMEM((T, R), f32),
+            pltpu.VMEM((T, R), bf16),
+            pltpu.VMEM((L, R), f32),
+            pltpu.VMEM((KVH, T, DH), f32),
+            pltpu.VMEM((KVH, T, DH), f32),
+            pltpu.VMEM((8, DH), f32),
+        ],
+        compiler_params=pltpu.CompilerParams(vmem_limit_bytes=60 * 2**20),
+    )(q, g, kn, vv, kr, qg, kg, live, ln)
+
+
+def reduce_kernel(dk, dv, raw, kg, part, pk, pv, gains, acc_k, acc_v, gbuf, hbuf, gs, gr, hs, hr, *scratch):
+    keys = Stream(True, acc_k, pk, *scratch[:6])
+    values = Stream(False, acc_v, pv, *scratch[6:])
+    greet(pltpu.get_barrier_semaphore(), others("resp", RESPS), others("group", GROUPS))
+    me, group = lax.axis_index("resp"), lax.axis_index("group")
+    gain = kg[...]
+    terms = []
+
+    def finish_keys(h, s):
+        rows = s.rows(s.shard, SHARD)
+        g, term = norm_grad(acc_k[h, rows, :].astype(f32), raw[h].astype(f32), gain)
+        pk[h, rows, :] = g.astype(bf16)
+        terms.append(term)
+
+    def finish_values(h, s):
+        rows = s.rows(s.shard, SHARD)
+        pv[h, rows, :] = acc_v[h, rows, :]
+
+    for h in range(KVH):
+        acc_k[h] = dk[h]
+        acc_v[h] = dv[h]
+        keys.phase(h, 0, None)
+        values.phase(h, 0, None)
+    small = []
+    for t in range(1, PHASES + KVH - 1):
+        for h in range(KVH):
+            if 1 <= t - h < PHASES:
+                keys.phase(h, t - h, finish_keys)
+                values.phase(h, t - h, finish_values)
+        if t == 4 + KVH - 1:
+            extra = jnp.sum(sum(terms), axis=0, keepdims=True)
+            row = lax.broadcasted_iota(jnp.int32, (8, DH), 0)
+            gbuf[me] = part[...] + jnp.where(row == 1, extra, 0.0)
+            small = exchange("resp", RESPS, gbuf, gs, gr)
+        if t == 4 + KVH + 1:
+            for one in small:
+                one.wait()
+            hbuf[group] = gbuf[...].sum(0)
+            small = exchange("group", GROUPS, hbuf, hs, hr)
+    for one in small:
+        one.wait()
+    gains[...] = hbuf[...].sum(0) * (1.0 / (RESPS * GROUPS))
+
+
+def reduce(dk, dv, raw, kg, part):
+    vm = pl.BlockSpec(memory_space=pltpu.VMEM)
+    return pl.pallas_call(
+        reduce_kernel,
+        out_shape=(
+            jax.ShapeDtypeStruct((KVH, PROMPT, DH), bf16),
+            jax.ShapeDtypeStruct((KVH, PROMPT, DH), bf16),
+            jax.ShapeDtypeStruct((8, DH), f32),
+        ),
+        in_specs=[vm] * 5,
+        out_specs=(vm,) * 3,
+        scratch_shapes=[
+            pltpu.VMEM((KVH, PROMPT, DH), bf16),
+            pltpu.VMEM((KVH, PROMPT, DH), bf16),
+            pltpu.VMEM((RESPS, 8, DH), f32),
+            pltpu.VMEM((GROUPS, 8, DH), f32),
+            pltpu.SemaphoreType.DMA((RESPS - 1,)),
+            pltpu.SemaphoreType.DMA((RESPS - 1,)),
+            pltpu.SemaphoreType.DMA((GROUPS - 1,)),
+            pltpu.SemaphoreType.DMA((GROUPS - 1,)),
+            *stream_scratch(True),
+            *stream_scratch(False),
+        ],
+        compiler_params=pltpu.CompilerParams(
+            collective_id=1, has_side_effects=True, vmem_limit_bytes=56 * 2**20),
+    )(dk, dv, raw, kg, part)
 
 
 def spread(value, axis, root):
@@ -16,7 +500,7 @@
 
 def normalize(raw, gain):
     values = raw.astype(jnp.float32).reshape(raw.shape[0], -1, DH)
-    inverse = lax.rsqrt(jnp.mean(values * values, axis=-1, keepdims=True) + epsilon)
+    inverse = lax.rsqrt(jnp.mean(values * values, axis=-1, keepdims=True) + EPS)
     unit = values * inverse
     return (unit, inverse, (unit * gain).astype(jnp.bfloat16))
 
@@ -90,7 +574,7 @@
     return (grad_queries, jnp.moveaxis(grad_keys, 0, 1), jnp.moveaxis(grad_values, 0, 1))
 
 
-def body(
+def plain(
     query_raw,
     key_raw,
     response_values,
@@ -150,6 +634,28 @@
     )
 
 
+def fast(query_raw, key_raw, response_values, prompt_keys, prompt_values, grad_output, query_gain, key_gain,
+         lengths, owner):
+    is_leader = lax.axis_index("resp") == owner[0]
+    mine = is_leader.astype(jnp.int32).reshape(1, 1)
+    qg, kg = query_gain.reshape(1, DH), key_gain.reshape(1, DH)
+    kr = key_raw[0, 0]
+    kn, vv, raw, live = gather(prompt_keys[0, 0], prompt_values[0, 0], kr, response_values[0, 0], kg, mine, lengths)
+    qo, ko, vo, dk, dv, part = attend(query_raw[0, 0], grad_output[0, 0], kn, vv, kr, qg, kg, live, lengths)
+    pk, pv, gains = reduce(dk, dv, raw, kg, part)
+
+    def placed(x):
+        rows = jnp.moveaxis(x, 0, 1).reshape(PROMPT, KVH * DH)
+        return jnp.where(is_leader, rows, jnp.zeros((), bf16))[None, None]
+
+    return qo[None, None], ko[None, None], vo[None, None], placed(pk), placed(pv), gains[:2]
+
+
+def body(*args):
+    bound = DH ** 0.5 * jnp.max(jnp.abs(args[6] * args[7]))
+    return lax.cond(bound <= SAFE, fast, plain, *args)
+
+
 def solution(mesh):
     in_specs = (
         P("group", "resp", None, None),

time: 1060 us -> 1070 us (level); the launches traced: 1050 us -> 1050 us
    another operation x32 -> x40, local copies, waits for them, and re-layouts: 61.5 us -> 80 us
    cond x0 -> x44, local copies, waits for them, and re-layouts: none -> 12.5 us  [the longest x4 9.86 us: body(): return lax.cond(bound <= SAFE, fast, plain, *args)]
    another operation x17 -> x18, other arithmetic: 22.5 us -> 23 us
  transfers between devices with their start and end apart: 2 -> 2, of which waited for: 1 -> 1; matrix products, arithmetic and copies ran while one was open for 6% -> 4% of each run, Pallas kernels for 0% -> 0%
where the time goes in v1:
time: 1070 us; the launch traced here: 1050 us
  matrix products  341 us (32%)
  blocking collectives  242 us (23%)
  local copies, waits for them, and re-layouts  202 us (19%)
  other arithmetic  113 us (11%)
  waiting for transfers between devices  83.8 us (8%)
  loops' own time  51 us (5%)
  between operations  15.2 us (1%)
    psum x1, blocking collectives, plain(): key_total, value_total = lax.psum((key_sum, value_sum), 'resp')  144 us
    psum x1, waiting for transfers between devices, spread(): return lax.psum(jnp.where(mine, value, jnp.zeros_like(value)), axis)  83.7 us
    another operation x40, local copies, waits for them, and re-layouts  80 us
    dot_general x16, matrix products, one_pair(): jnp.einsum('rhd,kd->hrk', out_pair, value_block, preferred_element_type=j...  70.8 us
    sub x16, matrix products, one_pair(): exponent = jnp.exp(scores - peak)  69.5 us
    psum x1, blocking collectives, plain(): lax.psum(jnp.stack([query_part, key_part]), ('group', 'resp'))  68.3 us
    dot_general x16, matrix products, one_pair(): jnp.einsum('hrk,rhd->kd', grad_scores, query_pair, preferred_element_type...  63.1 us
    dot_general x16, matrix products, one_pair(): jnp.einsum('hrk,rhd->kd', probs_low, out_pair, preferred_element_type=jnp...  57.5 us
  transfers between devices with their start and end apart: 2, of which 1 were waited for; matrix products, arithmetic and copies ran while one was open for 4% of the time, Pallas kernels for 0%

profile of v1, /device:TPU:1, one launch (start us, length us, event | category | flops | bytes accessed | tf_op | source)
XLA Modules:
  0.0 1049.4 jit_solution(17969051464176719342)
XLA Ops:
  9.1 1032.3 %conditional.1 = (bf16[1,1,256,512]{3,2,1,0:T(8,128)(2,1)S(1)}, f32[2,128]{1,0:T(2,128)S(1)}, bf16[1,1,256,4096]{3,2,1,0:T(8,128)(2,1)}, bf16[1,1,256,512]{3,2,1...) conditional(s32[]{:T(128)} %convert_element_type.121, ...), branch_computations={%region_1.24_spmd, %region_24.25_spmd} | conditional | flops 1686852224 | bytes 350521728 | solution.py:656
  15.0 3.8 copy.87
  23.3 30.0 %psum.38 = f32[1,1]{1,0:T(1,128)} all-reduce(f32[1,1]{1,0:T(1,128)S(6)} %convert_element_type.112), channel_id=1, replica_groups=mesh['group'=8,'resp'=16] {'resp'}, use_global_device_ids=true, to_apply=%region_3.3 | all-reduce | flops 1 | bytes 8 | tf_op jit(solution)/shard_map/cond/branch_0_fun/psum | solution.py:595
  62.5 4.1 copy.97
  76.3 83.7 %all-reduce.7.cloned.1.call-done = (bf16[1792,512]{0,1:T(8,128)(2,1)}, bf16[1792,4,128]{2,0,1:T(8,128)(2,1)}) async-done(((bf16[1792,512]{0,1:T(8,128)(2,1)}, bf16[1792,4,128]{2,0,1:T(8,128)(2,1)}), (bf16[1792,512]{0,1:T(8,128)(2,1)}, bf16[1792,4,128]{2,0,1:T(8,128)(2,1)})) %all-reduce.7.cloned.1.call-update) | async-done | bytes 3670032 | tf_op jit(solution)/shard_map/cond/branch_0_fun/psum | solution.py:498
  162.0 4.0 copy.85
  176.6 594.4 %while.18 = (s32[]{:T(128)}, f32[4,2048,128]{1,2,0:T(8,128)}, f32[4,2048,128]{2,1,0:T(8,128)}, f32[16,256,2,128]{1,3,2,0:T(8,128)}, s32[16]{0:T(128)}, /*index=5...) while((s32[]{:T(128)}, f32[4,2048,128]{1,2,0:T(8,128)}, ...), condition=%wide.region_13.13_spmd.clone, body=%wide.region_8.12_spmd.clone.sunk | while | flops 1623918080 | bytes 42360708 | solution.py:570
  180.9 4.3 fusion.124
  190.9 4.4 fusion.127
  200.6 3.9 fusion.128
  218.0 4.3 fusion.124
  228.0 4.4 fusion.127
  237.7 3.9 fusion.128
  255.2 4.3 fusion.124
  265.2 4.4 fusion.127
  274.9 3.9 fusion.128
  292.4 4.3 fusion.124
  302.4 4.4 fusion.127
  312.1 3.9 fusion.128
  329.5 4.3 fusion.124
  339.5 4.4 fusion.127
  349.2 3.9 fusion.128
  366.7 4.3 fusion.124
  376.7 4.4 fusion.127
  386.4 3.9 fusion.128
  403.8 4.3 fusion.124
  413.8 4.4 fusion.127
  423.5 3.9 fusion.128
  440.9 4.3 fusion.124
  450.9 4.4 fusion.127
  460.6 3.9 fusion.128
  478.0 4.3 fusion.124
  488.0 4.4 fusion.127
  497.7 3.9 fusion.128
  515.2 4.3 fusion.124
  525.2 4.4 fusion.127
  534.9 3.9 fusion.128
  552.3 4.3 fusion.124
  562.3 4.4 fusion.127
  572.0 3.9 fusion.128
  589.5 4.3 fusion.124
  599.4 4.4 fusion.127
  609.2 3.9 fusion.128
  626.6 4.3 fusion.124
  636.6 4.4 fusion.127
  646.3 3.9 fusion.128
  663.8 4.3 fusion.124
  673.7 4.4 fusion.127
  683.5 3.9 fusion.128
  700.9 4.3 fusion.124
  710.9 4.4 fusion.127
  720.6 3.9 fusion.128
  738.0 4.3 fusion.124
  748.0 4.4 fusion.127
  757.7 3.9 fusion.128
  771.0 4.3 slice.56
  776.5 4.2 slice.57
  783.9 5.1 fusion.63
  796.1 5.2 copy.95
  801.3 144.1 %all-reduce.8 = bf16[1792,512]{0,1:T(8,128)(2,1)} all-reduce(f32[1792,512]{0,1:T(8,128)} %bitcast.252), channel_id=1, replica_groups=mesh['group'=8,'resp'=16] {'resp'}, use_global_device_ids=true, to_apply=%region_18.18 | all-reduce | flops 917504 | bytes 5505024 | tf_op jit(solution)/shard_map/cond/branch_0_fun/psum | solution.py:616
  948.3 5.2 copy.94
  953.4 4.4 multiply_reduce_fusion.1
  960.5 3.8 copy.117
  967.0 68.3 %psum.41 = f32[2,128]{1,0:T(2,128)S(1)} all-reduce(f32[2,128]{1,0:T(2,128)S(1)} %pad_maximum_fusion.2), channel_id=1, replica_groups=mesh['group'=8,'resp'=16] {'group','resp'}, use_global_device_ids=true, to_apply=%region_23.23 | all-reduce | flops 256 | bytes 2048 | tf_op jit(solution)/shard_map/cond/branch_0_fun/psum | solution.py:624
  (310 shorter events, 409.5 us)
Async XLA Ops:
  9.1 151.0 %all-reduce.7.cloned.1.call-start = ((), (), s32[]{:S(2)}) async-start(), calls=%async_computation.1 | async-start | bytes 7340032 | tf_op jit(solution)/shard_map/cond/branch_0_fun/psum | solution.py:498
  13.6 5.2 copy-start.6
  21.2 32.1 %copy-start.7 = (bf16[1,1,256,512]{3,2,1,0:T(8,128)(2,1)S(1)}, bf16[1,1,256,512]{3,2,1,0:T(8,128)(2,1)}, u32[]{:S(2)}) copy-start(bf16[1,1,256,512]{3,2,1,0:T(8,128)(2,1)} %get-tuple-element.347) | copy-start | bytes 786436 | tf_op jit(solution)/shard_map/cond
  21.2 32.3 %copy-start.19 = (f32[128]{0:T(128)S(1)}, f32[128]{0:T(128)}, u32[]{:S(2)}) copy-start(f32[128]{0:T(128)} %get-tuple-element.191) | copy-start | bytes 1540 | tf_op jit(solution)/shard_map/cond
  22.6 31.3 %copy-start.10 = (bf16[1,1,256,512]{3,2,1,0:T(8,128)(2,1)S(1)}, bf16[1,1,256,512]{3,2,1,0:T(8,128)(2,1)}, u32[]{:S(2)}) copy-start(bf16[1,1,256,512]{3,2,1,0:T(8,128)(2,1)} %get-tuple-element.349) | copy-start | bytes 786436 | tf_op jit(solution)/shard_map/cond
  22.6 925.7 %all-reduce.5.cloned.1.call-start = ((), (), s32[]{:S(2)}) async-start(), calls=%async_computation | async-start | bytes 7340032 | tf_op jit(solution)/shard_map/cond/branch_0_fun/psum | solution.py:616
  57.4 15.2 %copy-start = (bf16[1,1,256,4096]{2,3,1,0:T(8,128)(2,1)}, bf16[1,1,256,4096]{2,3,1,0:T(8,128)(2,1)S(1)}, u32[]{:S(2)}) copy-start(bf16[1,1,256,4096]{2,3,1,0:T(8,128)(2,1)S(1)} %copy.96) | copy-start | bytes 6291460 | tf_op jit(solution)/shard_map/cond
  59.9 8.6 copy-start.21
  62.5 10.2 copy-start.15
  62.5 10.2 copy-start.13
  162.0 6.8 copy-start.11
  166.0 2.8 copy-start.9
  780.7 3.2 copy-start.14
  780.7 3.2 copy-start.22
  789.0 0.8 copy-start.16
  789.1 1.6 copy-start.1
  789.1 2.8 copy-start.4
  789.1 2.8 copy-start.18
  948.3 5.2 copy-start.12
  953.4 4.4 copy-start.2
  953.4 4.8 copy-start.3
  953.4 4.8 copy-start.24
  1041.4 0.7 copy-start.17
  1041.4 0.7 copy-start.25
Sparse Core Ops, SparseCore 0:
  22.7 137.3 all-reduce.6
  781.9 165.9 all-reduce.4

commit v2 on v0

v2 whole, which is shorter than its diff:
```python
import functools
import math

import jax
import jax.numpy as jnp
from jax import lax
from jax.experimental import pallas as pl
from jax.experimental.pallas import tpu as pltpu
from jax.sharding import PartitionSpec as P

DH = 128
KVH = 4
QH = 32
L = 256
PROMPT = 1792
T = PROMPT + L
RESPS = 16
GROUPS = 8
EPS = 1e-6
HP = 2
R = HP * L
STEPS = QH // HP
PER = STEPS // KVH
FACT = DH ** -0.5
C2 = FACT * math.log2(math.e)
SUB = 256
AC = 1024
CH = 1024
SAFE = 60.0
f32 = jnp.float32
bf16 = jnp.bfloat16
MESH = pl.DeviceIdType.MESH


def dot(a, b):
    return jnp.dot(a, b, preferred_element_type=f32)


def fold8(x):
    return x.reshape(x.shape[0] // 8, 8, x.shape[1]).sum(0)


def unit_of(x):
    inv = lax.rsqrt(jnp.mean(x * x, axis=-1, keepdims=True) + EPS)
    return x * inv, inv


def norm_grad(grad, raw, gain):
    unit, inv = unit_of(raw)
    du = grad * gain
    return (du - unit * jnp.mean(du * unit, axis=-1, keepdims=True)) * inv, fold8(grad * unit)


HALF = PROMPT // 2
SHARD = PROMPT // 16


def place():
    me = lax.axis_index("resp")
    return me // 4, (me // 2) % 2, me % 2


CHIPS = [(dz, dx) for dz in range(4) for dx in range(2) if (dz, dx) != (0, 0)]
NEAR = len(CHIPS)


class Stream:
    def __init__(self, acc, dst, flat, r0, rd, send, recv):
        z, x, c = place()
        self.acc, self.dst, self.flat, self.r0, self.rd, self.send, self.recv = acc, dst, flat, r0, rd, send, recv
        self.half = c * HALF
        self.other_half = (1 - c) * HALF
        self.sib = z * 4 + x * 2 + (1 - c)
        self.spots = [((z + dz) % 4) * 2 + (x + dx) % 2 for dz, dx in CHIPS]
        self.peers = [spot * 2 + c for spot in self.spots]
        self.shard = self.half + (z * 2 + x) * SHARD

    def copy(self, h, slot, src, dst, who):
        return pltpu.make_async_remote_copy(
            src_ref=src, dst_ref=dst, send_sem=self.send.at[h, slot], recv_sem=self.recv.at[h, slot],
            device_id={"resp": who}, device_id_type=MESH)

    def rows(self, start, n):
        return pl.ds(pl.multiple_of(start, 16), n)

    def place(self, h, start, n):
        if self.flat:
            return self.dst.at[self.rows(start, n), pl.ds(h * DH, DH)]
        return self.dst.at[h, self.rows(start, n), :]

    def copies(self, h, k):
        a = self.acc
        if k == 0:
            return [self.copy(h, 0, a.at[h, self.rows(self.other_half, HALF), :], self.r0.at[h], self.sib)]
        if k == 1:
            return [
                self.copy(h, 1 + i, a.at[h, self.rows(self.half + self.spots[i] * SHARD, SHARD), :],
                          self.rd.at[h, i], self.peers[i])
                for i in range(NEAR)]
        if k == 2:
            r = self.place(h, self.shard, SHARD)
            return [self.copy(h, 1 + NEAR + i, r, r, self.peers[i]) for i in range(NEAR)]
        r = self.place(h, self.half, HALF)
        return [self.copy(h, 1 + 2 * NEAR, r, r, self.sib)]

    def phase(self, h, k, finish):
        if k > 0:
            for one in self.copies(h, k - 1):
                one.wait()
        if k == 1:
            rows = self.rows(self.half, HALF)
            self.acc[h, rows, :] = (self.acc[h, rows, :].astype(f32) + self.r0[h].astype(f32)).astype(bf16)
        if k == 2:
            total = self.acc[h, self.rows(self.shard, SHARD), :].astype(f32)
            for i in range(NEAR):
                total = total + self.rd[h, i].astype(f32)
            finish(h, self, total)
        if k < 4:
            for one in self.copies(h, k):
                one.start()


PHASES = 5


def stream_scratch():
    return [
        pltpu.VMEM((KVH, HALF, DH), bf16),
        pltpu.VMEM((KVH, NEAR, SHARD, DH), bf16),
        pltpu.SemaphoreType.DMA((KVH, 2 + 2 * NEAR)),
        pltpu.SemaphoreType.DMA((KVH, 2 + 2 * NEAR)),
    ]


def greet(barrier, peers_resp, peers_group):
    for p in peers_resp:
        pl.semaphore_signal(barrier, inc=1, device_id={"resp": p}, device_id_type=MESH)
    for p in peers_group:
        pl.semaphore_signal(barrier, inc=1, device_id={"group": p}, device_id_type=MESH)
    pl.semaphore_wait(barrier, len(peers_resp) + len(peers_group))


def others(axis, n):
    me = lax.axis_index(axis)
    return [(me + d) % n for d in range(1, n)]


def exchange(axis, n, buf, send, recv):
    me = lax.axis_index(axis)
    copies = [
        pltpu.make_async_remote_copy(
            src_ref=buf.at[me], dst_ref=buf.at[me], send_sem=send.at[d - 1], recv_sem=recv.at[d - 1],
            device_id={axis: (me + d) % n}, device_id_type=MESH)
        for d in range(1, n)]
    for one in copies:
        one.start()
    return copies


def gather_kernel(kp, vp, kr, vr, kg, mine, ln, kn, vv, raw, live, acc_k, acc_v, lbuf, lsend, lrecv, *scratch):
    keys = Stream(acc_k, kn, False, *scratch[:4])
    values = Stream(acc_v, vv, False, *scratch[4:])
    greet(pltpu.get_barrier_semaphore(), others("resp", RESPS), [])
    me = lax.axis_index("resp")
    lbuf[me] = jnp.zeros((8, DH), f32) + ln[0, 0].astype(f32)
    small = exchange("resp", RESPS, lbuf, lsend, lrecv)
    gain = kg[...]

    def finish_keys(h, s, x):
        raw[h] = x.astype(bf16)
        unit, _ = unit_of(x)
        kn[h, s.rows(s.shard, SHARD), :] = (unit * gain).astype(bf16)

    def finish_values(h, s, x):
        vv[h, s.rows(s.shard, SHARD), :] = x.astype(bf16)

    flag = mine[0, 0] > 0
    for h in range(KVH):
        cols = slice(h * DH, (h + 1) * DH)
        acc_k[h] = jnp.where(flag, kp[:, cols], jnp.zeros((), bf16))
        acc_v[h] = jnp.where(flag, vp[:, cols], jnp.zeros((), bf16))
        keys.phase(h, 0, None)
        values.phase(h, 0, None)
    for h in range(KVH):
        cols = slice(h * DH, (h + 1) * DH)
        unit, _ = unit_of(kr[:, cols].astype(f32))
        kn[h, PROMPT:, :] = (unit * gain).astype(bf16)
        vv[h, PROMPT:, :] = vr[:, cols]
    for t in range(1, PHASES + KVH - 1):
        for h in range(KVH):
            if 1 <= t - h < PHASES:
                keys.phase(h, t - h, finish_keys)
                values.phase(h, t - h, finish_values)
    for one in small:
        one.wait()
    live[...] = lbuf[...].sum(0)


def gather(kp, vp, kr, vr, kg, mine, ln):
    vm, sm = pl.BlockSpec(memory_space=pltpu.VMEM), pl.BlockSpec(memory_space=pltpu.SMEM)
    return pl.pallas_call(
        gather_kernel,
        out_shape=(
            jax.ShapeDtypeStruct((KVH, T, DH), bf16),
            jax.ShapeDtypeStruct((KVH, T, DH), bf16),
            jax.ShapeDtypeStruct((KVH, SHARD, DH), bf16),
            jax.ShapeDtypeStruct((8, DH), f32),
        ),
        in_specs=[vm] * 5 + [sm] * 2,
        out_specs=(vm,) * 4,
        scratch_shapes=[
            pltpu.VMEM((KVH, PROMPT, DH), bf16),
            pltpu.VMEM((KVH, PROMPT, DH), bf16),
            pltpu.VMEM((RESPS, 8, DH), f32),
            pltpu.SemaphoreType.DMA((RESPS - 1,)),
            pltpu.SemaphoreType.DMA((RESPS - 1,)),
            *stream_scratch(),
            *stream_scratch(),
        ],
        compiler_params=pltpu.CompilerParams(
            collective_id=1, has_side_effects=True, vmem_limit_bytes=56 * 2**20),
    )(kp, vp, kr, vr, kg, mine, ln)


def prepare(h, q_ref, g_ref, gain, live, qt, gt):
    cols = pl.ds(pl.multiple_of(h * DH, DH), DH)
    rows = pl.ds(pl.multiple_of((h % HP) * L, L), L)
    unit, _ = unit_of(q_ref[:, cols].astype(f32))
    qt[h // HP, :, rows] = (unit * gain).T.astype(bf16)
    gt[h // HP, :, rows] = (g_ref[:, cols].astype(f32) * live).T.astype(bf16)


def front_chunk(c, kh, q, g, shift, kn, vv, eb, dp, bias, l, rd):
    x = dot(kn[kh, c * AC:(c + 1) * AC, :], q)
    y = dot(vv[kh, c * AC:(c + 1) * AC, :], g)
    for b in range(AC // SUB):
        lo = c * AC + b * SUB
        rows = slice(lo, lo + SUB)
        xs = x[b * SUB:(b + 1) * SUB] * C2 - shift
        if lo >= PROMPT:
            xs = xs + bias[lo - PROMPT:lo - PROMPT + SUB, :]
        ys = y[b * SUB:(b + 1) * SUB]
        e = jnp.exp2(xs)
        eb[rows, :] = e.astype(bf16)
        dp[rows, :] = ys
        l = l + fold8(e)
        rd = rd + fold8(e * ys)
    return l, rd


def front_end(l, rd):
    inv = 1.0 / jnp.sum(l, axis=0, keepdims=True)
    return inv, jnp.sum(rd, axis=0, keepdims=True) * inv


def back_begin(s, inv, qt, gt):
    return (qt[s].astype(f32) * inv).T.astype(bf16), (gt[s].astype(f32) * inv).T.astype(bf16)


def back_chunk(c, first, kh, slot, rd, q, g, knt, eb, dp, ds, dk, dv, acc):
    rows = slice(c * CH, (c + 1) * CH)
    add_v = dot(eb[rows, :], g)
    for b in range(CH // SUB):
        r = slice(c * CH + b * SUB, c * CH + (b + 1) * SUB)
        ds[r, :] = (eb[r, :].astype(f32) * (dp[r, :] - rd)).astype(bf16)
    low = ds[rows, :]
    add_k = dot(low, q)
    if first:
        dv[slot, rows, :] = add_v
        dk[slot, rows, :] = add_k
    else:
        dv[slot, rows, :] += add_v
        dk[slot, rows, :] += add_k
    t = dot(knt[kh, :, rows], low)
    return t if acc is None else acc + t


def finish_query(s, dqt, q_ref, gain, out, gpart):
    for half in range(HP):
        cols = pl.ds(pl.multiple_of((s * HP + half) * DH, DH), DH)
        grad, term = norm_grad(dqt[:, half * L:(half + 1) * L].T, q_ref[:, cols].astype(f32), gain)
        out[:, cols] = grad.astype(bf16)
        gpart[...] += term


TABLE = [
    [(0, [("in", 1, 2)]), (1, [("out", 0, 0), ("in", 3, 1)]), (2, [("out", 1, 0), ("in", 3, 3)]),
     (3, [("out", 2, 0), ("out", 0, 4)])],
    [(0, [("in", 2, 1)]), (1, [("in", 2, 3), ("out", 0, 1)]), (2, [("out", 1, 1)]),
     (3, [("out", 2, 1), ("out", 1, 3)])],
    [(0, [("in", 1, 3)]), (1, [("in", 3, 2)]), (2, [("in", 3, 4), ("out", 0, 3)]), (3, [("out", 1, 4)])],
    [(0, [("in", 1, 4), ("in", 2, 2)]), (1, [("in", 2, 4), ("out", 0, 2)]), (2, [("out", 1, 2)]),
     (3, [("out", 2, 2)])],
]


def main_kernel(q_hbm, g_hbm, kp, vp, kr, vr, qg, kg, shift, mine, ln,
                qo, ko, vo, pk, pv, gains,
                q_ref, g_ref, acc_k, acc_v, kn, vv, raw, knt, qt, gt, eb0, eb1, dp0, dp1, ds, bias, dk, dv,
                gpart, kpart, lbuf, gbuf, hbuf, load, lsend, lrecv, gs, gr, hs, hr, *scratch):
    in_k = Stream(acc_k, kn, False, *scratch[0:4])
    in_v = Stream(acc_v, vv, False, *scratch[4:8])
    out_k = Stream(acc_k, pk, True, *scratch[8:12])
    out_v = Stream(acc_v, pv, True, *scratch[12:16])
    me, group = lax.axis_index("resp"), lax.axis_index("group")
    q_gain, k_gain = qg[...], kg[...]

    loads = []
    for h in range(KVH):
        cols = pl.ds(h * DH, DH)
        loads.append(pltpu.make_async_copy(kp.at[:, cols], acc_k.at[h], load.at[2 * h]))
        loads.append(pltpu.make_async_copy(vp.at[:, cols], acc_v.at[h], load.at[2 * h + 1]))
    loads.append(pltpu.make_async_copy(g_hbm, g_ref, load.at[2 * KVH]))
    loads.append(pltpu.make_async_copy(q_hbm, q_ref, load.at[2 * KVH + 1]))
    for one in loads:
        one.start()
    lbuf[me] = jnp.zeros((8, DH), f32) + ln[0, 0].astype(f32)
    greet(pltpu.get_barrier_semaphore(), others("resp", RESPS), others("group", GROUPS))
    small = exchange("resp", RESPS, lbuf, lsend, lrecv)

    def shard_in_keys(h, s, x):
        raw[h] = x.astype(bf16)
        unit, _ = unit_of(x)
        kn[h, s.rows(s.shard, SHARD), :] = (unit * k_gain).astype(bf16)

    def shard_in_values(h, s, x):
        vv[h, s.rows(s.shard, SHARD), :] = x.astype(bf16)

    def shard_out_keys(h, s, x):
        grad, term = norm_grad(x, raw[h].astype(f32), k_gain)
        pk[s.rows(s.shard, SHARD), h * DH:(h + 1) * DH] = grad.astype(bf16)
        kpart[...] += term

    def shard_out_values(h, s, x):
        pv[s.rows(s.shard, SHARD), h * DH:(h + 1) * DH] = x.astype(bf16)

    def bring(h, k):
        in_k.phase(h, k, shard_in_keys)
        in_v.phase(h, k, shard_in_values)

    def send_back(h, k):
        out_k.phase(h, k, shard_out_keys)
        out_v.phase(h, k, shard_out_values)

    def turn(h):
        for b in range(0, T, 256):
            knt[h, :, b:b + 256] = kn[h, b:b + 256, :].astype(f32).T.astype(bf16)

    def close_head(h, slot):
        cols = pl.ds(pl.multiple_of(h * DH, DH), DH)
        grad, term = norm_grad(dk[slot, PROMPT:, :] * FACT, kr[:, cols].astype(f32), k_gain)
        ko[:, cols] = grad.astype(bf16)
        vo[:, cols] = dv[slot, PROMPT:, :].astype(bf16)
        kpart[...] += term
        acc_k[h] = (dk[slot, :PROMPT, :] * FACT).astype(bf16)
        acc_v[h] = dv[slot, :PROMPT, :].astype(bf16)

    flag = mine[0, 0] > 0
    for h in range(KVH):
        loads[2 * h].wait()
        loads[2 * h + 1].wait()
        acc_k[h] = jnp.where(flag, acc_k[h], jnp.zeros((), bf16))
        acc_v[h] = jnp.where(flag, acc_v[h], jnp.zeros((), bf16))
        bring(h, 0)
    for h in range(KVH):
        cols = slice(h * DH, (h + 1) * DH)
        unit, _ = unit_of(kr[:, cols].astype(f32))
        kn[h, PROMPT:, :] = (unit * k_gain).astype(bf16)
        vv[h, PROMPT:, :] = vr[:, cols]
    key_row = lax.broadcasted_iota(jnp.int32, (L, R), 0)
    query_row = lax.broadcasted_iota(jnp.int32, (L, R), 1) % L
    bias[...] = jnp.where(key_row <= query_row, 0.0, -1e30)
    gpart[...] = jnp.zeros_like(gpart)
    kpart[...] = jnp.zeros_like(kpart)
    bring(0, 1)
    for one in small:
        one.wait()
    scale = RESPS * L / lbuf[...].sum(0)[0:1, 0:1]
    live = jnp.where(lax.broadcasted_iota(jnp.int32, (L, 1), 0) < ln[0, 0], scale, 0.0)
    loads[2 * KVH].wait()
    loads[2 * KVH + 1].wait()

    def prep(h, _):
        prepare(h, q_ref, g_ref, q_gain, live, qt, gt)
        return 0
    lax.fori_loop(0, QH // 2, prep, 0)
    bring(0, 2)
    lax.fori_loop(QH // 2, QH, prep, 0)
    bring(0, 3)
    bring(1, 1)
    bring(0, 4)

    ebs, dps = (eb0, eb1), (dp0, dp1)
    l = rd = jnp.zeros((8, R), f32)
    for c in range(T // AC):
        l, rd = front_chunk(c, 0, qt[0], gt[0], shift[0], kn, vv, eb0, dp0, bias, l, rd)

    def one_head(kh, carry):
        inv, rd = carry
        slot = kh % 2
        turn(kh)
        for j in range(PER):
            for head, work in TABLE[j]:
                @pl.when(kh == head)
                def _():
                    for act, h, k in work:
                        if act == "in":
                            bring(h, k)
                        else:
                            if k == 0:
                                close_head(h, h % 2)
                            send_back(h, k)

            s = PER * kh + j + 1
            sn = jnp.minimum(s, STEPS - 1)
            prev, now = j % 2, 1 - j % 2
            q2, g2 = back_begin(s - 1, inv, qt, gt)
            q, g, m = qt[sn], gt[sn], shift[sn]
            l = r = jnp.zeros((8, R), f32)
            acc = None
            for c in range(T // AC):
                l, r = front_chunk(c, sn // PER, q, g, m, kn, vv, ebs[now], dps[now], bias, l, r)
                acc = back_chunk(c, j == 0, kh, slot, rd, q2, g2, knt, ebs[prev], dps[prev], ds, dk, dv, acc)
            finish_query(s - 1, acc * (inv * FACT), q_ref, q_gain, qo, gpart)
            inv, rd = front_end(l, r)
        return inv, rd
    lax.fori_loop(0, KVH, one_head, front_end(l, rd))

    close_head(KVH - 1, (KVH - 1) % 2)
    send_back(KVH - 1, 0)
    send_back(KVH - 1, 1)
    send_back(KVH - 2, 3)
    send_back(KVH - 1, 2)
    row = lax.broadcasted_iota(jnp.int32, (8, DH), 0)
    query_term = jnp.sum(gpart[...], axis=0, keepdims=True)
    key_term = jnp.sum(kpart[...], axis=0, keepdims=True)
    gbuf[me] = jnp.where(row == 0, query_term, 0.0) + jnp.where(row == 1, key_term, 0.0)
    small = exchange("resp", RESPS, gbuf, gs, gr)
    send_back(KVH - 2, 4)
    for one in small:
        one.wait()
    hbuf[group] = gbuf[...].sum(0)
    small = exchange("group", GROUPS, hbuf, hs, hr)
    send_back(KVH - 1, 3)
    send_back(KVH - 1, 4)
    for one in small:
        one.wait()
    gains[...] = hbuf[...].sum(0)[:2] * (1.0 / (RESPS * GROUPS))


def attend(q, g, kp, vp, kr, vr, qg, kg, shift, mine, ln):
    vm, sm = pl.BlockSpec(memory_space=pltpu.VMEM), pl.BlockSpec(memory_space=pltpu.SMEM)
    hbm = pl.BlockSpec(memory_space=pl.ANY)
    whole = jax.ShapeDtypeStruct((PROMPT, KVH * DH), bf16)
    pair = lambda n: [pltpu.SemaphoreType.DMA((n,)), pltpu.SemaphoreType.DMA((n,))]
    return pl.pallas_call(
        main_kernel,
        out_shape=(
            jax.ShapeDtypeStruct((L, QH * DH), bf16),
            jax.ShapeDtypeStruct((L, KVH * DH), bf16),
            jax.ShapeDtypeStruct((L, KVH * DH), bf16),
            whole, whole,
            jax.ShapeDtypeStruct((2, DH), f32),
        ),
        in_specs=[hbm] * 4 + [vm] * 5 + [sm] * 2,
        out_specs=(vm,) * 6,
        scratch_shapes=[
            pltpu.VMEM((L, QH * DH), bf16),
            pltpu.VMEM((L, QH * DH), bf16),
            pltpu.VMEM((KVH, PROMPT, DH), bf16),
            pltpu.VMEM((KVH, PROMPT, DH), bf16),
            pltpu.VMEM((KVH, T, DH), bf16),
            pltpu.VMEM((KVH, T, DH), bf16),
            pltpu.VMEM((KVH, SHARD, DH), bf16),
            pltpu.VMEM((KVH, DH, T), bf16),
            pltpu.VMEM((STEPS, DH, R), bf16),
            pltpu.VMEM((STEPS, DH, R), bf16),
            pltpu.VMEM((T, R), bf16),
            pltpu.VMEM((T, R), bf16),
            pltpu.VMEM((T, R), f32),
            pltpu.VMEM((T, R), f32),
            pltpu.VMEM((T, R), bf16),
            pltpu.VMEM((L, R), f32),
            pltpu.VMEM((2, T, DH), f32),
            pltpu.VMEM((2, T, DH), f32),
            pltpu.VMEM((8, DH), f32),
            pltpu.VMEM((8, DH), f32),
            pltpu.VMEM((RESPS, 8, DH), f32),
            pltpu.VMEM((RESPS, 8, DH), f32),
            pltpu.VMEM((GROUPS, 8, DH), f32),
            pltpu.SemaphoreType.DMA((2 * KVH + 2,)),
            *pair(RESPS - 1), *pair(RESPS - 1), *pair(GROUPS - 1),
            *stream_scratch(), *stream_scratch(), *stream_scratch(), *stream_scratch(),
        ],
        compiler_params=pltpu.CompilerParams(
            collective_id=0, has_side_effects=True, vmem_limit_bytes=63 * 2**20),
    )(q, g, kp, vp, kr, vr, qg, kg, shift, mine, ln)


def row_shifts(query, key, prompt_keys, prompt_values, values, qg, kg, mine, ln):
    kn, _, _, _ = gather(prompt_keys, prompt_values, key, values, kg, mine, ln)
    unit, _ = unit_of(query.astype(f32).reshape(L, QH, DH))
    qn = jnp.moveaxis((unit * qg).astype(bf16), 1, 0)
    seen = jnp.arange(T)[None, :] - PROMPT <= jnp.arange(L)[:, None]

    def one(h):
        q = lax.dynamic_index_in_dim(qn, h, 0, keepdims=False)
        k = lax.dynamic_index_in_dim(kn, h // (QH // KVH), 0, keepdims=False)
        scores = jnp.einsum("rd,kd->rk", q, k, preferred_element_type=f32)
        return jnp.max(jnp.where(seen, scores, -jnp.inf), axis=-1)
    return lax.map(one, jnp.arange(QH)).reshape(STEPS, 1, R) * C2


def body(query_raw, key_raw, response_values, prompt_keys, prompt_values, grad_output, query_gain, key_gain,
         lengths, owner):
    is_leader = lax.axis_index("resp") == owner[0]
    mine = is_leader.astype(jnp.int32).reshape(1, 1)
    qg, kg = query_gain.reshape(1, DH), key_gain.reshape(1, DH)
    q, g, kr, vr = query_raw[0, 0], grad_output[0, 0], key_raw[0, 0], response_values[0, 0]
    kp, vp = prompt_keys[0, 0], prompt_values[0, 0]
    bound = DH ** 0.5 * jnp.max(jnp.abs(query_gain * key_gain))
    shift = lax.cond(
        bound <= SAFE, lambda *_: jnp.zeros((STEPS, 1, R), f32), row_shifts,
        q, kr, kp, vp, vr, qg, kg, mine, lengths)
    qo, ko, vo, pk, pv, gains = attend(q, g, kp, vp, kr, vr, qg, kg, shift, mine, lengths)

    def placed(x):
        return jnp.where(is_leader, x, jnp.zeros((), bf16))[None, None]

    return qo[None, None], ko[None, None], vo[None, None], placed(pk), placed(pv), gains


def solution(mesh):
    in_specs = (
        P("group", "resp", None, None),
        P("group", "resp", None, None),
        P("group", "resp", None, None),
        P("group", "resp", None, None),
        P("group", "resp", None, None),
        P("group", "resp", None, None),
        P(),
        P(),
        P("group", "resp"),
        P("group"),
    )
    out_specs = (
        P("group", "resp", None, None),
        P("group", "resp", None, None),
        P("group", "resp", None, None),
        P("group", "resp", None, None),
        P("group", "resp", None, None),
        P(),
    )
    return jax.shard_map(body, mesh=mesh, in_specs=in_specs, out_specs=out_specs, check_vma=False)
```

time: 1060 us -> 385 us (0.36)
  matrix products: 339 us -> 44.2 us
  blocking collectives: 249 us -> 0 us
  local copies, waits for them, and re-layouts: 210 us -> 28 us
  Pallas kernels: 0 us -> 175 us
  other arithmetic: 122 us -> 5.92 us
  loops' own time: 42.4 us -> 126 us
  waiting for transfers between devices: 74.9 us -> 0 us
  between operations: 16.4 us -> 2.61 us
    psum x3 -> x0, blocking collectives: 249 us -> none  [the longest x1 147 us: body(): key_total, value_total = lax.psum((key_sum, value_sum), 'resp')]
    dot_general x80 -> x32, matrix products: 270 us -> 44.2 us  [one(): scores = jnp.einsum('rd,kd->rk', q, k, preferred_element_type=f32)]
    pallas_call x0 -> x2, Pallas kernels: none -> 175 us  [the longest x1 116 us: attend(): pl.pallas_call(main_kernel, out_shape=(jax.ShapeDtypeStruct((L, QH * DH),...]
    another operation x1 -> x2, loops' own time: 42.4 us -> 126 us  [the longest x1 125 us: row_shifts(): return lax.map(one, jnp.arange(QH)).reshape(STEPS, 1, R) * C2]
    psum x2 -> x0, waiting for transfers between devices: 74.8 us -> none  [the longest x1 74.8 us: spread(): return lax.psum(jnp.where(mine, value, jnp.zeros_like(value)), axis)]
    sub x16 -> x0, matrix products: 69.6 us -> none  [one_pair(): exponent = jnp.exp(scores - peak)]
    another operation x32 -> x1, local copies, waits for them, and re-layouts: 61.5 us -> 3.28 us
    convert_element_type x21 -> x0, other arithmetic: 50.6 us -> none  [the longest x16 40.6 us: one_pair(): probs_low = probs.astype(jnp.bfloat16)]
  transfers between devices with their start and end apart: 2 -> 0, of which waited for: 1 -> 0; matrix products, arithmetic and copies ran while one was open for 6% -> 0% of each run, Pallas kernels for 0% -> 0%
where the time goes in v2:
time: 385 us; the launch traced here: 382 us
  Pallas kernels  175 us (45%)
  loops' own time  126 us (33%)
  matrix products  44.2 us (11%)
  local copies, waits for them, and re-layouts  28 us (7%)
  other arithmetic  5.92 us (2%)
    another operation x1, loops' own time, row_shifts(): return lax.map(one, jnp.arange(QH)).reshape(STEPS, 1, R) * C2  125 us
    pallas_call x1, Pallas kernels, attend(): pl.pallas_call(main_kernel, out_shape=(jax.ShapeDtypeStruct((L, QH * DH),...  116 us
    pallas_call x1, Pallas kernels, gather(): pl.pallas_call(gather_kernel, out_shape=(jax.ShapeDtypeStruct((KVH, T, DH...  59 us
    dot_general x32, matrix products, one(): scores = jnp.einsum('rd,kd->rk', q, k, preferred_element_type=f32)  44.2 us
    dynamic_slice x32, local copies, waits for them, and re-layouts, row_shifts(): return lax.map(one, jnp.arange(QH)).reshape(STEPS, 1, R) * C2  18.8 us

profile of v2, /device:TPU:1, one launch (start us, length us, event | category | flops | bytes accessed | tf_op | source)
XLA Modules:
  0.0 381.7 jit_solution(3515618859854639155)
XLA Ops:
  1.9 1.3 abs_reduce_fusion
  3.9 255.7 %conditional.1 = (f32[16,1,512]{2,1,0:T(1,128)S(1)}) conditional(s32[]{:T(128)} %convert_element_type.8, (bf16[256,4096]{1,0:T(8,128)(2,1)}, f32[128]{0:T(128)}, bf16[1792,512]{1,0:T(8,128)(2,1)}, bf16[1792,512]{1,0:T(8,128)(2,1)}, bf16[256,512]{1,0:T(8,128)(2,1)}, /*index=5*/bf16[256,512]{1,0:T(8,128)(2,1)}, f32[1,128]{1,0:T(1,128)}, ...), branch_computations={%region_1.6_spmd, %region_6.7_spmd} | conditional | flops 143148816 | bytes 28139790 | solution.py:522
  3.9 3.3 copy.18
  7.9 2.1 fusion.11
  9.9 0.7 copy-done.1
  10.7 59.0 %branch_0_fun.1 = (bf16[4,2048,128]{2,1,0:T(8,128)(2,1)S(1)}, bf16[4,2048,128]{2,1,0:T(8,128)(2,1)}, bf16[4,112,128]{2,1,0:T(8,128)(2,1)}, f32[8,128]{1,0:T(8,128)}) custom-call(bf16[1792,512]{1,0:T(8,128)(2,1)S(1)} %copy-done, bf16[1792,512]{1,0:T(8,128)(2,1)S(1)} %copy-done.1, bf16[256,512]{1,0:T(8,128)(2,1)S(1)} %copy-done.3, ...), custom_call_target="tpu_custom_call" | custom-call | tf_op jit(solution)/shard_map/cond/branch_0_fun/pallas_call | solution.py:201
  69.8 189.7 %while.12 = (s32[]{:T(128)}, f32[32,256]{1,0:T(8,128)S(1)}, s32[32]{0:T(128)S(1)}, bf16[32,256,128]{1,2,0:T(8,128)(2,1)}, bf16[4,2048,128]{2,1,0:T(8,128)(2,1)S(...) while((s32[]{:T(128)}, f32[32,256]{1,0:T(8,128)S(1)}, ...), condition=%wide.region_5.5_spmd.clone, body=%wide.region_3.4_spmd.clone.sunk | while | flops 135790352 | bytes 601454 | solution.py:511
  69.8 0.6 dynamic_slice.37
  74.3 1.4 fusion.17
  75.7 0.6 dynamic_slice.37
  80.2 1.4 fusion.17
  81.6 0.6 dynamic_slice.37
  86.1 1.4 fusion.17
  87.6 0.6 dynamic_slice.37
  92.1 1.4 fusion.17
  93.5 0.6 dynamic_slice.37
  98.0 1.4 fusion.17
  99.5 0.6 dynamic_slice.37
  103.9 1.4 fusion.17
  105.4 0.6 dynamic_slice.37
  109.9 1.4 fusion.17
  111.3 0.6 dynamic_slice.37
  115.8 1.4 fusion.17
  117.2 0.6 dynamic_slice.37
  121.7 1.4 fusion.17
  123.2 0.6 dynamic_slice.37
  127.7 1.4 fusion.17
  129.1 0.6 dynamic_slice.37
  133.6 1.4 fusion.17
  135.0 0.6 dynamic_slice.37
  139.5 1.4 fusion.17
  141.0 0.6 dynamic_slice.37
  145.4 1.4 fusion.17
  146.9 0.6 dynamic_slice.37
  151.4 1.4 fusion.17
  152.8 0.6 dynamic_slice.37
  157.3 1.4 fusion.17
  163.2 1.4 fusion.17
  169.2 1.4 fusion.17
  175.1 1.4 fusion.17
  181.0 1.4 fusion.17
  182.5 0.6 dynamic_slice.37
  186.9 1.4 fusion.17
  188.4 0.6 dynamic_slice.37
  192.9 1.4 fusion.17
  194.3 0.6 dynamic_slice.37
  198.8 1.4 fusion.17
  200.2 0.6 dynamic_slice.37
  204.7 1.4 fusion.17
  206.2 0.6 dynamic_slice.37
  210.7 1.4 fusion.17
  216.6 1.4 fusion.17
  222.5 1.4 fusion.17
  228.4 1.4 fusion.17
  234.4 1.4 fusion.17
  240.3 1.4 fusion.17
  246.2 1.4 fusion.17
  252.2 1.4 fusion.17
  258.1 1.4 fusion.17
  259.6 116.4 %shard_map.145 = (bf16[256,4096]{1,0:T(8,128)(2,1)}, bf16[256,512]{1,0:T(8,128)(2,1)}, bf16[256,512]{1,0:T(8,128)(2,1)}, bf16[1792,512]{1,0:T(8,128)(2,1)}, bf16[1792,512]{1,0:T(8,128)(2,1)}, /*index=5*/f32[2,128]{1,0:T(2,128)}) custom-call(bf16[256,4096]{1,0:T(8,128)(2,1)} %bitcast.42, bf16[256,4096]{1,0:T(8,128)(2,1)} %bitcast.47, ...), custom_call_target="tpu_custom_call" | custom-call | tf_op jit(solution)/shard_map/pallas_call | solution.py:456
  376.0 2.1 select_bitcast_fusion
  378.4 1.3 copy.38
  379.8 0.7 copy.39
  380.5 0.7 copy.40
  (71 shorter events, 10.0 us)
Async XLA Ops:
  7.2 0.7 copy-start.7
  7.8 2.1 copy-start
  7.8 2.8 copy-start.1
  7.9 2.8 copy-start.3
  7.9 2.9 copy-start.4
  7.9 2.9 copy-start.8
  376.0 2.5 copy-start.2
  378.4 1.3 copy-start.6
  378.4 2.0 copy-start.5
  378.4 2.7 copy-start.9

commit v3 on v2

--- a/solution.py
+++ b/solution.py
@@ -283,20 +283,25 @@
         gpart[...] += term
 
 
-TABLE = [
-    [(0, [("in", 1, 2)]), (1, [("out", 0, 0), ("in", 3, 1)]), (2, [("out", 1, 0), ("in", 3, 3)]),
-     (3, [("out", 2, 0), ("out", 0, 4)])],
-    [(0, [("in", 2, 1)]), (1, [("in", 2, 3), ("out", 0, 1)]), (2, [("out", 1, 1)]),
-     (3, [("out", 2, 1), ("out", 1, 3)])],
-    [(0, [("in", 1, 3)]), (1, [("in", 3, 2)]), (2, [("in", 3, 4), ("out", 0, 3)]), (3, [("out", 1, 4)])],
-    [(0, [("in", 1, 4), ("in", 2, 2)]), (1, [("in", 2, 4), ("out", 0, 2)]), (2, [("out", 1, 2)]),
-     (3, [("out", 2, 2)])],
-]
+TABLE = {
+    0: [("in", 1, 2), ("in", 2, 1)],
+    2: [("in", 1, 3)],
+    3: [("in", 1, 4), ("in", 2, 2), ("in", 3, 1)],
+    4: [("out", 0, 0)],
+    6: [("in", 2, 3), ("in", 3, 2), ("out", 0, 1)],
+    7: [("in", 2, 4)],
+    8: [("out", 1, 0)],
+    9: [("in", 3, 3), ("out", 0, 2), ("out", 1, 1)],
+    10: [("in", 3, 4)],
+    12: [("out", 0, 3), ("out", 1, 2), ("out", 2, 0)],
+    13: [("out", 0, 4), ("out", 2, 1)],
+    15: [("out", 1, 3)],
+}
 
 
 def main_kernel(q_hbm, g_hbm, kp, vp, kr, vr, qg, kg, shift, mine, ln,
-                qo, ko, vo, pk, pv, gains,
-                q_ref, g_ref, acc_k, acc_v, kn, vv, raw, knt, qt, gt, eb0, eb1, dp0, dp1, ds, bias, dk, dv,
+                qo_hbm, ko, vo, pk, pv, gains,
+                qo, q_ref, g_ref, acc_k, acc_v, kn, vv, raw, knt, qt, gt, eb0, eb1, dp0, dp1, ds, bias, dk, dv,
                 gpart, kpart, lbuf, gbuf, hbuf, load, lsend, lrecv, gs, gr, hs, hr, *scratch):
     in_k = Stream(acc_k, kn, False, *scratch[0:4])
     in_v = Stream(acc_v, vv, False, *scratch[4:8])
@@ -326,10 +331,21 @@
     def shard_in_values(h, s, x):
         vv[h, s.rows(s.shard, SHARD), :] = x.astype(bf16)
 
+    shared = []
+
     def shard_out_keys(h, s, x):
         grad, term = norm_grad(x, raw[h].astype(f32), k_gain)
         pk[s.rows(s.shard, SHARD), h * DH:(h + 1) * DH] = grad.astype(bf16)
         kpart[...] += term
+        if isinstance(h, int) and h == KVH - 1:
+            shared.extend(share_gains())
+
+    def share_gains():
+        row = lax.broadcasted_iota(jnp.int32, (8, DH), 0)
+        query_term = jnp.sum(gpart[...], axis=0, keepdims=True)
+        key_term = jnp.sum(kpart[...], axis=0, keepdims=True)
+        gbuf[me] = jnp.where(row == 0, query_term, 0.0) + jnp.where(row == 1, key_term, 0.0)
+        return exchange("resp", RESPS, gbuf, gs, gr)
 
     def shard_out_values(h, s, x):
         pv[s.rows(s.shard, SHARD), h * DH:(h + 1) * DH] = x.astype(bf16)
@@ -400,11 +416,14 @@
         slot = kh % 2
         turn(kh)
         for j in range(PER):
-            for head, work in TABLE[j]:
-                @pl.when(kh == head)
+            for n, work in TABLE.items():
+                if n % PER != j:
+                    continue
+
+                @pl.when(kh == n // PER)
                 def _():
-                    for act, h, k in work:
-                        if act == "in":
+                    for way, h, k in work:
+                        if way == "in":
                             bring(h, k)
                         else:
                             if k == 0:
@@ -426,16 +445,16 @@
         return inv, rd
     lax.fori_loop(0, KVH, one_head, front_end(l, rd))
 
+    keep = pltpu.make_async_copy(qo, qo_hbm, load.at[0])
+    keep.start()
     close_head(KVH - 1, (KVH - 1) % 2)
     send_back(KVH - 1, 0)
+    send_back(KVH - 2, 2)
     send_back(KVH - 1, 1)
+    send_back(KVH - 3, 4)
     send_back(KVH - 2, 3)
     send_back(KVH - 1, 2)
-    row = lax.broadcasted_iota(jnp.int32, (8, DH), 0)
-    query_term = jnp.sum(gpart[...], axis=0, keepdims=True)
-    key_term = jnp.sum(kpart[...], axis=0, keepdims=True)
-    gbuf[me] = jnp.where(row == 0, query_term, 0.0) + jnp.where(row == 1, key_term, 0.0)
-    small = exchange("resp", RESPS, gbuf, gs, gr)
+    small = shared
     send_back(KVH - 2, 4)
     for one in small:
         one.wait()
@@ -443,8 +462,11 @@
     small = exchange("group", GROUPS, hbuf, hs, hr)
     send_back(KVH - 1, 3)
     send_back(KVH - 1, 4)
+    pk[...] = jnp.where(flag, pk[...], jnp.zeros((), bf16))
+    pv[...] = jnp.where(flag, pv[...], jnp.zeros((), bf16))
     for one in small:
         one.wait()
+    keep.wait()
     gains[...] = hbuf[...].sum(0)[:2] * (1.0 / (RESPS * GROUPS))
 
 
@@ -463,8 +485,9 @@
             jax.ShapeDtypeStruct((2, DH), f32),
         ),
         in_specs=[hbm] * 4 + [vm] * 5 + [sm] * 2,
-        out_specs=(vm,) * 6,
+        out_specs=(hbm,) + (vm,) * 5,
         scratch_shapes=[
+            pltpu.VMEM((L, QH * DH), bf16),
             pltpu.VMEM((L, QH * DH), bf16),
             pltpu.VMEM((L, QH * DH), bf16),
             pltpu.VMEM((KVH, PROMPT, DH), bf16),
@@ -524,10 +547,7 @@
         q, kr, kp, vp, vr, qg, kg, mine, lengths)
     qo, ko, vo, pk, pv, gains = attend(q, g, kp, vp, kr, vr, qg, kg, shift, mine, lengths)
 
-    def placed(x):
-        return jnp.where(is_leader, x, jnp.zeros((), bf16))[None, None]
-
-    return qo[None, None], ko[None, None], vo[None, None], placed(pk), placed(pv), gains
+    return qo[None, None], ko[None, None], vo[None, None], pk[None, None], pv[None, None], gains
 
 
 def solution(mesh):

time: 385 us -> 384 us (level)
  local copies, waits for them, and re-layouts: 28 us -> 32 us
    unnamed x12 -> x16, local copies, waits for them, and re-layouts: 3.67 us -> 7.72 us
where the time goes in v3:
time: 384 us; the launch traced here: 380 us
  Pallas kernels  172 us (45%)
  loops' own time  126 us (33%)
  matrix products  44.2 us (12%)
  local copies, waits for them, and re-layouts  32 us (8%)
    another operation x1, loops' own time, row_shifts(): return lax.map(one, jnp.arange(QH)).reshape(STEPS, 1, R) * C2  125 us
    pallas_call x1, Pallas kernels, attend(): pl.pallas_call(main_kernel, out_shape=(jax.ShapeDtypeStruct((L, QH * DH),...  113 us
    pallas_call x1, Pallas kernels, gather(): pl.pallas_call(gather_kernel, out_shape=(jax.ShapeDtypeStruct((KVH, T, DH...  59 us
    dot_general x32, matrix products, one(): scores = jnp.einsum('rd,kd->rk', q, k, preferred_element_type=f32)  44.2 us
    dynamic_slice x32, local copies, waits for them, and re-layouts, row_shifts(): return lax.map(one, jnp.arange(QH)).reshape(STEPS, 1, R) * C2  18.8 us
    unnamed x16, local copies, waits for them, and re-layouts  7.72 us

profile of v3, /device:TPU:1, one launch (start us, length us, event | category | flops | bytes accessed | tf_op | source)
XLA Modules:
  0.0 380.1 jit_solution(10196628362830089112)
XLA Ops:
  1.9 1.3 abs_reduce_fusion
  3.9 255.7 %conditional.1 = (f32[16,1,512]{2,1,0:T(1,128)S(1)}) conditional(s32[]{:T(128)} %convert_element_type.8, (bf16[256,4096]{1,0:T(8,128)(2,1)}, f32[128]{0:T(128)}, bf16[1792,512]{1,0:T(8,128)(2,1)}, bf16[1792,512]{1,0:T(8,128)(2,1)}, bf16[256,512]{1,0:T(8,128)(2,1)}, /*index=5*/bf16[256,512]{1,0:T(8,128)(2,1)}, f32[1,128]{1,0:T(1,128)}, ...), branch_computations={%region_1.6_spmd, %region_6.7_spmd} | conditional | flops 143148816 | bytes 28139790 | solution.py:545
  3.9 3.3 copy.18
  7.9 2.1 fusion.11
  9.9 0.7 copy-done.1
  10.7 59.0 %branch_0_fun.1 = (bf16[4,2048,128]{2,1,0:T(8,128)(2,1)S(1)}, bf16[4,2048,128]{2,1,0:T(8,128)(2,1)}, bf16[4,112,128]{2,1,0:T(8,128)(2,1)}, f32[8,128]{1,0:T(8,128)}) custom-call(bf16[1792,512]{1,0:T(8,128)(2,1)S(1)} %copy-done, bf16[1792,512]{1,0:T(8,128)(2,1)S(1)} %copy-done.1, bf16[256,512]{1,0:T(8,128)(2,1)S(1)} %copy-done.4, ...), custom_call_target="tpu_custom_call" | custom-call | tf_op jit(solution)/shard_map/cond/branch_0_fun/pallas_call | solution.py:201
  69.8 189.7 %while.12 = (s32[]{:T(128)}, f32[32,256]{1,0:T(8,128)S(1)}, s32[32]{0:T(128)S(1)}, bf16[32,256,128]{1,2,0:T(8,128)(2,1)}, bf16[4,2048,128]{2,1,0:T(8,128)(2,1)S(...) while((s32[]{:T(128)}, f32[32,256]{1,0:T(8,128)S(1)}, ...), condition=%wide.region_5.5_spmd.clone, body=%wide.region_3.4_spmd.clone.sunk | while | flops 135790352 | bytes 601454 | solution.py:534
  74.3 1.4 fusion.17
  75.7 0.6 dynamic_slice.37
  80.2 1.4 fusion.17
  81.6 0.6 dynamic_slice.37
  86.1 1.4 fusion.17
  87.6 0.6 dynamic_slice.37
  92.1 1.4 fusion.17
  93.5 0.6 dynamic_slice.37
  98.0 1.4 fusion.17
  99.5 0.6 dynamic_slice.37
  103.9 1.4 fusion.17
  105.4 0.6 dynamic_slice.37
  109.9 1.4 fusion.17
  111.3 0.6 dynamic_slice.37
  115.8 1.4 fusion.17
  117.2 0.6 dynamic_slice.37
  121.7 1.4 fusion.17
  123.2 0.6 dynamic_slice.37
  127.7 1.4 fusion.17
  129.1 0.6 dynamic_slice.37
  133.6 1.4 fusion.17
  135.0 0.6 dynamic_slice.37
  139.5 1.4 fusion.17
  141.0 0.6 dynamic_slice.37
  145.4 1.4 fusion.17
  151.4 1.4 fusion.17
  157.3 1.4 fusion.17
  163.2 1.4 fusion.17
  169.2 1.4 fusion.17
  170.6 0.6 dynamic_slice.37
  175.1 1.4 fusion.17
  176.5 0.6 dynamic_slice.37
  181.0 1.4 fusion.17
  182.5 0.6 dynamic_slice.37
  186.9 1.4 fusion.17
  188.4 0.6 dynamic_slice.37
  192.9 1.4 fusion.17
  194.3 0.6 dynamic_slice.37
  198.8 1.4 fusion.17
  200.2 0.6 dynamic_slice.37
  204.7 1.4 fusion.17
  206.2 0.6 dynamic_slice.37
  210.7 1.4 fusion.17
  216.6 1.4 fusion.17
  222.5 1.4 fusion.17
  228.4 1.4 fusion.17
  234.4 1.4 fusion.17
  240.3 1.4 fusion.17
  246.2 1.4 fusion.17
  252.2 1.4 fusion.17
  258.1 1.4 fusion.17
  259.6 112.8 %shard_map.145 = (bf16[256,4096]{1,0:T(8,128)(2,1)}, bf16[256,512]{1,0:T(8,128)(2,1)}, bf16[256,512]{1,0:T(8,128)(2,1)}, bf16[1792,512]{1,0:T(8,128)(2,1)}, bf16[1792,512]{1,0:T(8,128)(2,1)}, /*index=5*/f32[2,128]{1,0:T(2,128)}) custom-call(bf16[256,4096]{1,0:T(8,128)(2,1)} %bitcast.40, bf16[256,4096]{1,0:T(8,128)(2,1)} %bitcast.45, ...), custom_call_target="tpu_custom_call" | custom-call | tf_op jit(solution)/shard_map/pallas_call | solution.py:478
  372.4 3.3 copy.40
  375.7 0.7 copy.41
  376.4 0.7 copy.42
  377.1 1.2 copy.43
  378.3 1.2 copy.44
  (74 shorter events, 10.3 us)
Async XLA Ops:
  7.2 0.7 copy-start.8
  7.8 2.1 copy-start
  7.8 2.8 copy-start.1
  7.9 2.8 copy-start.4
  7.9 2.9 copy-start.5
  7.9 2.9 copy-start.9
  372.4 3.3 copy-start.7
  372.4 4.0 %copy-start.6 = (bf16[256,512]{1,0:T(8,128)(2,1)S(1)}, bf16[256,512]{1,0:T(8,128)(2,1)}, u32[]{:S(2)}) copy-start(bf16[256,512]{1,0:T(8,128)(2,1)} %get-tuple-element.123) | copy-start | bytes 786436
  372.4 4.7 %copy-start.3 = (bf16[1792,512]{1,0:T(8,128)(2,1)S(1)}, bf16[1792,512]{1,0:T(8,128)(2,1)}, u32[]{:S(2)}) copy-start(bf16[1792,512]{1,0:T(8,128)(2,1)} %get-tuple-element.124) | copy-start | bytes 5505028
  376.4 1.9 copy-start.2
  378.3 1.2 copy-start.10
